TPU v7x, 512 devices: a whole 4x8x8 slice. The times are simulated.
512 devices in a mesh: brick: 64 (over y_hi, z, core), chan: 8 (over y_lo, x).
Axes of the slice: x: 4, y: 8 (y_hi: 4, y_lo: 2; y = y_hi * 2 + y_lo), z: 8, core: 2. Of those that a mesh axis runs over, the one named last changes fastest.
Arguments:
- features: bfloat16 [512, 32768], P('chan', 'brick'), may hold values from -6 to 6
- positions: float32 [3, 32768], P(None, 'brick'), may hold values from 0 to 1, as said below
- lists: int32 [256, 4], P('brick'), may hold values from 0 to 7, as said below
- counts: int32 [256], P('brick'), may hold values from 1 to 4, as said below
- fourier_filter: float32 [512, 4096], P('chan'), may hold values from 0.5 to 4
- radial_weights: float32 [8, 512], P(None, 'chan'), may hold values from -4 to 4
- norm_gain: float32 [512], replicated, may hold values from 0.1 to 1.9
- mlp_in: bfloat16 [1024, 512], P(None, 'chan'), may hold values from -0.25 to 0.25
- mlp_out: bfloat16 [512, 1024], P('chan'), may hold values from -0.1875 to 0.1875
Outputs:
- updated: bfloat16 [512, 32768], P(None, ('brick', 'chan'))
Inputs may be any that keep to these rules, and one draw needn't show every extreme that they name: Row g of lists holds 4 different values from (g mod 4) to (g mod 4) + 4. `counts`: the value 4 occurs in every draw. `positions`: for an atom of block j of its brick (j = its index // 128 mod 4) the first coordinate lies between j / 4 and (j + 1) / 4; the other two lie in [0, 1).
All inputs are finite; a program needn't handle non-finite values.
Results may differ from a plain program's by a relative error of at most 0.0055.
The roundings to bfloat16 on the way count: a program that leaves them out, or rounds other values in their place, can miss the bound.
Values may be sent and summed in bfloat16 or wider, within the bound.
A program may use at most 64 MiB of HBM per device.

v0:
```python
import math

import jax
import jax.numpy as jnp
from jax import lax
from jax.sharding import Mesh
from jax.sharding import PartitionSpec as P

KSIDE = 16
BLOCK = 128
BRICK = ("brick_0", "brick_1", "brick_2")
BRICK_CHAN = ("brick_0", "brick_1", "brick_2", "chan")


brick_width = 4.0
cross_width = 8.0
cutoff = 2.0
epsilon = 1e-06


def with_halo(cells, sides, width):
    for axis, dim in sides:
        count = lax.axis_size(axis)
        head = lax.slice_in_dim(cells, 0, width, axis=dim)
        tail = lax.slice_in_dim(cells, cells.shape[dim] - width, cells.shape[dim], axis=dim)
        cells = jnp.concatenate(
            [
                lax.ppermute(tail, axis, [(i, (i + 1) % count) for i in range(count)]),
                cells,
                lax.ppermute(head, axis, [((i + 1) % count, i) for i in range(count)]),
            ],
            axis=dim,
        )
    return cells


def cut_along(x, dim, size):
    before, after = (x.shape[:dim], x.shape[dim + 1 :])
    return jnp.moveaxis(x.reshape(*before, size, -1, *after), dim, 0)


def summed_on_arrival(x, axis, dim):
    pieces = cut_along(x, dim, lax.axis_size(axis))
    arrived = lax.all_to_all(pieces, axis, split_axis=0, concat_axis=0, tiled=True)
    return arrived.sum(axis=0)


def sum_by_axis(x, axes, dim):
    far, near = axes
    own = summed_on_arrival(cut_along(x, dim, lax.axis_size(far)), near, dim + 1)
    return jnp.sum(lax.all_to_all(own, far, 0, 0, tiled=True), axis=0)


def rows_for(lines, size):
    spare = -len(lines) % size
    return jnp.pad(lines, [(0, spare)] + [(0, 0)] * (lines.ndim - 1))


def sent_to_all(x, axis):
    size = lax.axis_size(axis)
    return lax.all_to_all(jnp.broadcast_to(x[None], (size, *x.shape)), axis, 0, 0, tiled=True)


def laid_out(pieces, dim):
    lengths = list(pieces.shape[1:])
    lengths[dim] *= pieces.shape[0]
    return jnp.moveaxis(pieces, 0, dim).reshape(lengths)


def whole_of(x, axes, dim):
    far, near = axes
    pieces = sent_to_all(sent_to_all(x, far), near)
    return laid_out(pieces.swapaxes(0, 1).reshape(-1, *x.shape), dim)


def nested_sum(x, axes):
    lines = x.reshape(-1, x.shape[-1])
    own = sum_by_axis(rows_for(lines, lax.axis_size(axes[0]) * lax.axis_size(axes[1])), axes, 0)
    whole = whole_of(own, axes, 0)
    return whole[: len(lines)].reshape(x.shape)


def gathered_copies(x, axis, dim):
    pieces = sent_to_all(x, axis)
    return laid_out(pieces, dim)


def wave_table(side_count, brick_count):
    wave_index = jnp.arange(side_count**3, dtype=jnp.int32)
    first_number = (wave_index % side_count + 1).astype(jnp.float32)
    second_number = (wave_index // side_count % side_count - side_count // 2).astype(jnp.float32)
    third_number = (wave_index // (side_count * side_count) - side_count // 2).astype(jnp.float32)
    along_x = first_number * (2.0 * math.pi / (brick_count * brick_width))
    along_y = second_number * (2.0 * math.pi / cross_width)
    along_z = third_number * (2.0 * math.pi / cross_width)
    return (along_x, along_y, along_z)


def angle_rows(places, brick_float, along_x, along_y, along_z):
    x_place = (brick_float + places[0]) * brick_width
    y_place = places[1] * cross_width
    z_place = places[2] * cross_width
    return (
        x_place[:, None] * along_x[None, :]
        + y_place[:, None] * along_y[None, :]
        + z_place[:, None] * along_z[None, :]
    )


def phase_rows(places, brick_float, wave_vectors):
    angles = angle_rows(places, brick_float, wave_vectors[0], wave_vectors[1], wave_vectors[2])
    return jnp.concatenate([jnp.cos(angles), jnp.sin(angles)], axis=1).astype(jnp.bfloat16)


def radial_basis(delta_x, delta_y, delta_z, basis_count):
    squared = delta_x * delta_x + delta_y * delta_y + delta_z * delta_z
    distance = jnp.sqrt(squared)
    envelope = jnp.square(jnp.maximum(1.0 - squared / (cutoff * cutoff), 0.0))
    spacing = cutoff / (basis_count - 1)
    centres = (jnp.arange(basis_count, dtype=jnp.float32) * spacing).reshape(
        (basis_count,) + (1,) * distance.ndim
    )
    scaled_gap = (distance[None] - centres) / spacing
    return (jnp.exp(-scaled_gap * scaled_gap) * envelope[None]).astype(jnp.bfloat16)


def body(
    features, positions, lists, counts, fourier_filter, radial_weights, norm_gain, mlp_in, mlp_out
):
    channels, atom_count = features.shape
    block_size = BLOCK
    blocks_dev = atom_count // block_size
    phase_step = min(256, atom_count)
    phase_turns = atom_count // phase_step
    rim_size = blocks_dev // 2 * block_size
    basis_count = radial_weights.shape[0]
    list_width = lists.shape[1]
    brick_count = lax.axis_size(BRICK)
    brick_float = lax.axis_index(BRICK).astype(jnp.float32)
    wave_vectors = wave_table(KSIDE, brick_count)
    inverse = 1.0 / math.sqrt(atom_count * brick_count)
    column_total = 2 * wave_vectors[0].shape[0]

    def add_block(step_index, partial_value):
        first_atom = step_index * phase_step
        places = lax.dynamic_slice_in_dim(positions, first_atom, phase_step, 1)
        feature_rows = lax.dynamic_slice_in_dim(features, first_atom, phase_step, 1)
        phases = phase_rows(places, brick_float, wave_vectors)
        return partial_value + jnp.dot(feature_rows, phases, preferred_element_type=jnp.float32)

    partial_value = lax.fori_loop(
        0, phase_turns, add_block, jnp.zeros((channels, column_total), jnp.float32)
    )
    feature_ext = with_halo(features, ((BRICK, 1),), rim_size)
    place_ext = with_halo(positions, ((BRICK, 1),), rim_size)
    ext_blocks = place_ext.shape[1] // block_size
    offsets = jnp.concatenate(
        [
            jnp.full((rim_size,), -1.0, jnp.float32),
            jnp.zeros((atom_count,), jnp.float32),
            jnp.ones((rim_size,), jnp.float32),
        ]
    )
    source_x_all = (place_ext[0] + offsets).reshape(ext_blocks, block_size)
    source_y_all = place_ext[1].reshape(ext_blocks, block_size)
    source_z_all = place_ext[2].reshape(ext_blocks, block_size)
    scaled_ext = (
        feature_ext[:, None, :].astype(jnp.float32) * radial_weights.T[:, :, None]
    ).astype(jnp.bfloat16)
    scaled_blocks = scaled_ext.reshape(channels, basis_count, ext_blocks, block_size)

    def target_places(target):
        target_first = target * block_size
        return [
            lax.dynamic_slice_in_dim(positions[axis_index], target_first, block_size)
            for axis_index in range(3)
        ]

    def one_target(target, messages):
        used_count = counts[target]
        list_row = lists[target]
        target_x, target_y, target_z = target_places(target)
        source_x = jnp.take(source_x_all, list_row, axis=0)
        source_y = jnp.take(source_y_all, list_row, axis=0)
        source_z = jnp.take(source_z_all, list_row, axis=0)
        radial_terms = radial_basis(
            (source_x[:, :, None] - target_x[None, None, :]) * brick_width,
            (source_y[:, :, None] - target_y[None, None, :]) * cross_width,
            (source_z[:, :, None] - target_z[None, None, :]) * cross_width,
            basis_count,
        )
        used_mask = (jnp.arange(list_width, dtype=jnp.int32) < used_count).astype(jnp.bfloat16)
        radial_terms = radial_terms * used_mask[None, :, None, None]
        source = jnp.take(scaled_blocks, list_row, axis=2)
        summed_block = jnp.dot(
            source.reshape(channels, basis_count * list_width * block_size),
            radial_terms.reshape(basis_count * list_width * block_size, block_size),
            preferred_element_type=jnp.float32,
        )
        return lax.dynamic_update_slice_in_dim(messages, summed_block, target * block_size, 1)

    messages = lax.fori_loop(
        0, blocks_dev, one_target, jnp.zeros((channels, atom_count), jnp.float32)
    )
    filter_both = jnp.concatenate([fourier_filter, fourier_filter], axis=1)
    summed = nested_sum(partial_value, (("brick_0", "brick_1"), "brick_2")) * inverse
    filtered = (filter_both * summed).astype(jnp.bfloat16)

    def eval_block(step_index, accumulated):
        first_atom = step_index * phase_step
        places = lax.dynamic_slice_in_dim(positions, first_atom, phase_step, 1)
        phases = phase_rows(places, brick_float, wave_vectors)
        contrib = lax.dot_general(
            filtered, phases, (((1,), (1,)), ((), ())), preferred_element_type=jnp.float32
        )
        return lax.dynamic_update_slice_in_dim(accumulated, contrib, first_atom, 1)

    ewald = (
        lax.fori_loop(0, phase_turns, eval_block, jnp.zeros((channels, atom_count), jnp.float32))
        * inverse
    )
    mixed = (features.astype(jnp.float32) + messages + ewald).astype(jnp.bfloat16)
    atom_rows = lax.all_to_all(mixed, "chan", split_axis=1, concat_axis=0, tiled=True)
    values = atom_rows.astype(jnp.float32)
    mean_square = jnp.mean(values * values, axis=0, keepdims=True)
    normed = (values * lax.rsqrt(mean_square + epsilon) * norm_gain[:, None]).astype(jnp.bfloat16)
    hidden = jnp.dot(gathered_copies(mlp_in, "chan", 1), normed, preferred_element_type=jnp.float32)
    active = jax.nn.gelu(hidden).astype(jnp.bfloat16)
    return (
        values
        + jnp.dot(gathered_copies(mlp_out, "chan", 0), active, preferred_element_type=jnp.float32)
    ).astype(jnp.bfloat16)


def solution(mesh):
    torus = Mesh(
        mesh.devices.reshape(4, 8, 2, mesh.shape["chan"]), ("brick_0", "brick_1", "brick_2", "chan")
    )
    return jax.shard_map(
        body,
        mesh=torus,
        in_specs=(
            P("chan", BRICK),
            P(None, BRICK),
            P(BRICK, None),
            P(BRICK),
            P("chan", None),
            P(None, "chan"),
            P(),
            P(None, "chan"),
            P("chan", None),
        ),
        out_specs=P(None, BRICK_CHAN),
        check_vma=False,
    )
```

profile of v0, /device:TPU:1, one launch (start us, length us, event | category | flops | bytes accessed | tf_op | source)
XLA Modules:
  0.0 228.0 jit_solution(18019023819246128166)
XLA Ops:
  0.0 43.1 %while.44 = (s32[]{:T(128)}, f32[64,8192]{1,0:T(8,128)}, bf16[64,512]{1,0:T(8,128)(2,1)}, f32[]{:T(128)}, f32[3,512]{1,0:T(4,128)}, /*index=5*/s32[]{:T(128)}, s...) while((s32[]{:T(128)}, f32[64,8192]{1,0:T(8,128)}, bf16[64,512]{1,0:T(8,128)(2,1)}, f32[]{:T(128)}, ...), condition=%wide.region_3.5_spmd.clone, body=%wide.region_2.4_spmd.clone.sunk | while | flops 285377536 | bytes 12985581 | solution.py:151
  0.0 0.9 fusion.165
  0.9 16.5 %cosine_convert_fusion.5 = (bf16[256,4096]{1,0:T(8,128)(2,1)S(1)}, bf16[256,4096]{1,0:T(8,128)(2,1)}) fusion(f32[4096]{0:T(1024)S(1)} %fusion.164, f32[256]{0:T(256)S(1)} %bitcast.144, f32[4096]{0:T(1024)S(1)} %get-tuple-element.745, f32[256]{0:T(256)S(1)} %bitcast.143, f32[4096]{0:T(1024)S(1)} %get-tuple-element.747, f32[256]{0:T(256)S(1)} %bitcast.142), kind=kLoop, calls=%fused_computation.58.clone.1 | loop fusion | flops 7340032 | bytes 4246528 | tf_op jit(solution)/shard_map/convert
  17.4 3.8 %convolution_add_fusion.2 = f32[64,8192]{1,0:T(8,128)} fusion(bf16[256,4096]{1,0:T(8,128)(2,1)} %get-tuple-element.749, bf16[256,4096]{1,0:T(8,128)(2,1)S(1)} %get-tuple-element.750, f32[64,8192]{1,0:T(8,128)} %get-tuple-element.763, pred[]{:T(512)S(6)} %compare.9, bf16[64,512]{1,0:T(8,128)(2,1)S(1)} %copy-done, s32[]{:T(128)S(6)} %select_n.392), kind=kOutput, calls=%fused_computation.53.clone.1 | convolution fusion | flops 277872640 | bytes 8421381 | tf_op jit(solution)/shard_map/while/body/eval_jaxpr/dot_general | solution.py:149
  21.2 0.9 fusion.165
  22.1 16.5 %cosine_convert_fusion.5 = (bf16[256,4096]{1,0:T(8,128)(2,1)S(1)}, bf16[256,4096]{1,0:T(8,128)(2,1)}) fusion(f32[4096]{0:T(1024)S(1)} %fusion.164, f32[256]{0:T(256)S(1)} %bitcast.144, f32[4096]{0:T(1024)S(1)} %get-tuple-element.745, f32[256]{0:T(256)S(1)} %bitcast.143, f32[4096]{0:T(1024)S(1)} %get-tuple-element.747, f32[256]{0:T(256)S(1)} %bitcast.142), kind=kLoop, calls=%fused_computation.58.clone.1 | loop fusion | flops 7340032 | bytes 4246528 | tf_op jit(solution)/shard_map/convert
  38.7 4.4 %convolution_add_fusion.2 = f32[64,8192]{1,0:T(8,128)} fusion(bf16[256,4096]{1,0:T(8,128)(2,1)} %get-tuple-element.749, bf16[256,4096]{1,0:T(8,128)(2,1)S(1)} %get-tuple-element.750, f32[64,8192]{1,0:T(8,128)} %get-tuple-element.763, pred[]{:T(512)S(6)} %compare.9, bf16[64,512]{1,0:T(8,128)(2,1)S(1)} %copy-done, s32[]{:T(128)S(6)} %select_n.392), kind=kOutput, calls=%fused_computation.53.clone.1 | convolution fusion | flops 277872640 | bytes 8421381 | tf_op jit(solution)/shard_map/while/body/eval_jaxpr/dot_general | solution.py:149
  43.1 2.5 %reshape_reshape.4 = f32[32,2,1,8192]{3,1,0,2:T(2,128)S(1)} reshape(f32[64,8192]{1,0:T(8,128)} %get-tuple-element.439) | data formatting | bytes 4194304 | tf_op jit(solution)/shard_map/reshape;reshape | solution.py:39
  45.6 2.6 %copy.23 = f32[2,32,1,8192]{3,1,2,0:T(8,128)} copy(f32[2,32,1,8192]{3,0,1,2:T(2,128)S(1)} %bitcast.133) | data formatting | bytes 4194304 | tf_op jit(solution)/shard_map/transpose | solution.py:39
  48.1 10.6 %all-to-all-start = ((f32[2,32,1,8192]{3,1,2,0:T(8,128)}), f32[2,32,1,8192]{3,1,2,0:T(8,128)S(1)}, u32[]{:S(2)}, u32[]{:S(2)}) async-start(f32[2,32,1,8192]{3,1,2,0:T(8,128)} %copy.23), calls=%async_computation | async-start | bytes 4194304 | tf_op jit(solution)/shard_map/all_to_all | solution.py:44
  58.8 2.5 %all-to-all-done = f32[2,32,1,8192]{3,1,2,0:T(8,128)S(1)} async-done(((f32[2,32,1,8192]{3,1,2,0:T(8,128)}), f32[2,32,1,8192]{3,1,2,0:T(8,128)S(1)}, u32[]{:S(2)}, u32[]{:S(2)}) %all-to-all-start) | async-done | bytes 2097184 | tf_op jit(solution)/shard_map/all_to_all | solution.py:44
  61.5 2.1 reduce_sum.30
  63.7 10.3 %all-to-all-start.1 = ((f32[32,1,8192]{2,1,0:T(1,128)}), f32[32,1,8192]{2,1,0:T(1,128)S(1)}, u32[]{:S(2)}, u32[]{:S(2)}) async-start(f32[32,1,8192]{2,1,0:T(1,128)} %reduce_sum.30), calls=%async_computation.1 | async-start | bytes 2097152 | tf_op jit(solution)/shard_map/all_to_all | solution.py:51
  74.0 4.0 %collective-permute-start.2 = (f32[3,256]{1,0:T(4,128)S(1)}, f32[3,256]{1,0:T(4,128)S(1)}, u32[]{:S(2)}, u32[]{:S(2)}) collective-permute-start(f32[3,256]{1,0:T(4,128)S(1)} %get-tuple-element.575), channel_id=1, source_target_pairs={{0,8},{8,16},{16,24},{24,32},{32,40},{40,48},{48,56},{56,64},{64,7... | collective-permute-start | bytes 9224 | tf_op jit(solution)/shard_map/ppermute | solution.py:28
  78.0 1.9 collective-permute-start.3
  79.9 3.6 %collective-permute-start = (bf16[64,256]{1,0:T(8,128)(2,1)S(1)}, bf16[64,256]{1,0:T(8,128)(2,1)S(1)}, u32[]{:S(2)}, u32[]{:S(2)}) collective-permute-start(bf16[64,256]{1,0:T(8,128)(2,1)S(1)} %get-tuple-element.569), channel_id=1, source_target_pairs={{0,8},{8,16},{16,24},{24,32},{32,40},{40,48},{48,56},{56,64},{64,7... | collective-permute-start | bytes 98312 | tf_op jit(solution)/shard_map/ppermute | solution.py:28
  83.6 4.7 %collective-permute-start.1 = (bf16[64,256]{1,0:T(8,128)(2,1)S(1)}, bf16[64,256]{1,0:T(8,128)(2,1)S(1)}, u32[]{:S(2)}, u32[]{:S(2)}) collective-permute-start(bf16[64,256]{1,0:T(8,128)(2,1)S(1)} %get-tuple-element.570), channel_id=1, source_target_pairs={{8,0},{16,8},{24,16},{32,24},{40,32},{48,40},{56,48},{64,56},{72,6... | collective-permute-start | bytes 98312 | tf_op jit(solution)/shard_map/ppermute | solution.py:30
  88.5 0.8 collective-permute-done.1
  89.4 14.5 %all-to-all-done.1 = f32[32,1,8192]{2,1,0:T(1,128)S(1)} async-done(((f32[32,1,8192]{2,1,0:T(1,128)}), f32[32,1,8192]{2,1,0:T(1,128)S(1)}, u32[]{:S(2)}, u32[]{:S(2)}) %all-to-all-start.1) | async-done | bytes 1048608 | tf_op jit(solution)/shard_map/all_to_all | solution.py:51
  103.9 0.7 reduce_sum.31
  104.6 1.9 broadcast_in_dim.126
  106.5 8.4 %all-to-all-start.2 = ((f32[32,1,8192]{2,1,0:T(1,128)}), f32[32,1,8192]{2,1,0:T(1,128)S(1)}, u32[]{:S(2)}, u32[]{:S(2)}) async-start(f32[32,1,8192]{2,1,0:T(1,128)} %broadcast_in_dim.126), calls=%async_computation.2 | async-start | bytes 2097152 | tf_op jit(solution)/shard_map/all_to_all | solution.py:61
  115.6 23.7 %while.42 = (s32[]{:T(128)}, f32[64,512]{1,0:T(8,128)}, s32[4,4]{1,0:T(4,128)S(1)}, f32[8,128]{1,0:T(8,128)S(1)}, f32[3,512]{1,0:T(4,128)S(1)}, /*index=5*/f32[8...) while((s32[]{:T(128)}, f32[64,512]{1,0:T(8,128)}, ...), condition=%wide.region_1.3_spmd.clone, body=%wide.region_0.2_spmd.clone.sunk | while | flops 73076280 | bytes 5071827 | solution.py:202
  118.0 0.7 gather_fusion.3
  120.0 1.5 fusion.155
  123.9 0.7 gather_fusion.3
  126.0 1.5 fusion.155
  129.8 0.7 gather_fusion.3
  131.9 1.5 fusion.155
  135.7 0.7 gather_fusion.3
  137.8 1.5 fusion.155
  139.3 7.3 %all-to-all-done.2 = f32[32,1,8192]{2,1,0:T(1,128)S(1)} async-done(((f32[32,1,8192]{2,1,0:T(1,128)}), f32[32,1,8192]{2,1,0:T(1,128)S(1)}, u32[]{:S(2)}, u32[]{:S(2)}) %all-to-all-start.2) | async-done | bytes 1048608 | tf_op jit(solution)/shard_map/all_to_all | solution.py:61
  147.3 5.8 %all_to_all.43 = f32[2,32,1,8192]{3,1,2,0:T(8,128)S(1)} all-to-all(f32[2,32,1,8192]{3,1,2,0:T(8,128)S(1)} %broadcast_in_dim.128), channel_id=1, replica_groups=mesh['brick_0'=4,'brick_1'=8,'brick_2'=2,'chan'=8] {'brick_2'}, dimensions={0} | all-to-all | bytes 4194304 | tf_op jit(solution)/shard_map/all_to_all | solution.py:61
  153.1 1.1 broadcast_in_dim.129
  154.2 4.6 %all-to-all-start.5 = ((bf16[8,1024,64]{1,2,0:T(8,128)(2,1)}), bf16[8,1024,64]{1,2,0:T(8,128)(2,1)S(1)}, u32[]{:S(2)}, u32[]{:S(2)}) async-start(bf16[8,1024,64]{1,2,0:T(8,128)(2,1)} %broadcast_in_dim.129), calls=%async_computation.5 | async-start | bytes 2097152 | tf_op jit(solution)/shard_map/all_to_all | solution.py:61
  159.0 1.6 copy.24
  160.6 2.4 %mul.594 = f32[64,8192]{1,0:T(8,128)} reshape(f32[32,2,1,8192]{3,1,0,2:T(2,128)S(1)} %copy.24) | data formatting | bytes 4194304 | tf_op jit(solution)/shard_map/mul | solution.py:206
  163.1 2.4 %fusion.85 = bf16[64,8192]{1,0:T(8,128)(2,1)S(1)} fusion(f32[64,8192]{1,0:T(8,128)} %mul.594, f32[64,4096]{1,0:T(8,128)} %param.21), kind=kLoop, calls=%fused_computation.133 | loop fusion | flops 1572864 | bytes 4194304 | tf_op jit(solution)/shard_map/convert_element_type | solution.py:207
  165.5 34.6 %while.43 = (s32[]{:T(128)}, f32[64,512]{1,0:T(8,128)S(1)}, f32[]{:T(128)}, f32[3,512]{1,0:T(4,128)S(1)}, bf16[64,8192]{1,0:T(8,128)(2,1)S(1)}, /*index=5*/s32[]...) while((s32[]{:T(128)}, f32[64,512]{1,0:T(8,128)S(1)}, f32[]{:T(128)}, ...), condition=%wide.region_7.9_spmd.clone, body=%wide.region_6.8_spmd.clone.sunk | while | flops 284328960 | bytes 9610439 | solution.py:219
  165.6 15.8 %cosine_convert_fusion.4 = (bf16[256,4096]{1,0:T(8,128)(2,1)S(1)}, bf16[256,4096]{1,0:T(8,128)(2,1)S(1)}) fusion(f32[4096]{0:T(1024)S(1)} %fusion.158, f32[256]{0:T(256)S(1)} %bitcast.147, f32[4096]{0:T(1024)S(1)} %get-tuple-element.733, f32[256]{0:T(256)S(1)} %bitcast.146, f32[4096]{0:T(1024)S(1)} %get-tuple-element.735, f32[256]{0:T(256)S(1)} %bitcast.145), kind=kLoop, calls=%fused_computation.16.clone.1 | loop fusion | flops 7340032 | bytes 4246528 | tf_op jit(solution)/shard_map/convert.2
  181.4 1.4 fusion.161
  182.9 15.8 %cosine_convert_fusion.4 = (bf16[256,4096]{1,0:T(8,128)(2,1)S(1)}, bf16[256,4096]{1,0:T(8,128)(2,1)S(1)}) fusion(f32[4096]{0:T(1024)S(1)} %fusion.158, f32[256]{0:T(256)S(1)} %bitcast.147, f32[4096]{0:T(1024)S(1)} %get-tuple-element.733, f32[256]{0:T(256)S(1)} %bitcast.146, f32[4096]{0:T(1024)S(1)} %get-tuple-element.735, f32[256]{0:T(256)S(1)} %bitcast.145), kind=kLoop, calls=%fused_computation.16.clone.1 | loop fusion | flops 7340032 | bytes 4246528 | tf_op jit(solution)/shard_map/convert.2
  198.7 1.4 fusion.161
  200.5 10.1 %all_to_all.44 = bf16[8,2,2048]{2,1,0:T(2,128)(2,1)S(1)} all-to-all(bf16[8,2,2048]{2,1,0:T(2,128)(2,1)S(1)} %reshape.274), channel_id=1, replica_groups=mesh['brick_0'=4,'brick_1'=8,'brick_2'=2,'chan'=8] {'chan'}, dimensions={0} | all-to-all | bytes 131072 | tf_op jit(solution)/shard_map/all_to_all | solution.py:223
  210.6 1.1 broadcast_in_dim.130
  211.7 3.6 %all-to-all-start.6 = ((bf16[8,64,1024]{2,1,0:T(8,128)(2,1)}), bf16[8,64,1024]{2,1,0:T(8,128)(2,1)S(1)}, u32[]{:S(2)}, u32[]{:S(2)}) async-start(bf16[8,64,1024]{2,1,0:T(8,128)(2,1)} %broadcast_in_dim.130), calls=%async_computation.6 | async-start | bytes 2097152 | tf_op jit(solution)/shard_map/all_to_all | solution.py:61
  215.9 10.7 %all-to-all-done.6 = bf16[8,64,1024]{2,1,0:T(8,128)(2,1)S(1)} async-done(((bf16[8,64,1024]{2,1,0:T(8,128)(2,1)}), bf16[8,64,1024]{2,1,0:T(8,128)(2,1)S(1)}, u32[]{:S(2)}, u32[]{:S(2)}) %all-to-all-start.6) | async-done | bytes 1048608 | tf_op jit(solution)/shard_map/all_to_all | solution.py:61
  226.6 1.4 fusion.87
  (132 shorter events, 17.8 us)
Async XLA Ops:
  0.9 16.5 %copy-start = (bf16[64,512]{1,0:T(8,128)(2,1)S(1)}, bf16[64,512]{1,0:T(8,128)(2,1)}, u32[]{:S(2)}) copy-start(bf16[64,512]{1,0:T(8,128)(2,1)} %get-tuple-element.775) | copy-start | bytes 196612 | tf_op jit(solution)/shard_map/while
  22.1 16.5 %copy-start = (bf16[64,512]{1,0:T(8,128)(2,1)S(1)}, bf16[64,512]{1,0:T(8,128)(2,1)}, u32[]{:S(2)}) copy-start(bf16[64,512]{1,0:T(8,128)(2,1)} %get-tuple-element.775) | copy-start | bytes 196612 | tf_op jit(solution)/shard_map/while
  48.1 13.1 %all-to-all-start = ((f32[2,32,1,8192]{3,1,2,0:T(8,128)}), f32[2,32,1,8192]{3,1,2,0:T(8,128)S(1)}, u32[]{:S(2)}, u32[]{:S(2)}) async-start(f32[2,32,1,8192]{3,1,2,0:T(8,128)} %copy.23), calls=%async_computation | async-start | bytes 4194304 | tf_op jit(solution)/shard_map/all_to_all | solution.py:44
  61.5 12.5 %copy-start.2 = (f32[3,512]{1,0:T(4,128)S(1)}, f32[3,512]{1,0:T(4,128)}, u32[]{:S(2)}) copy-start(f32[3,512]{1,0:T(4,128)} %get-tuple-element.867) | copy-start | bytes 18436
  61.5 18.4 %copy-start.1 = (bf16[64,512]{1,0:T(8,128)(2,1)S(1)}, bf16[64,512]{1,0:T(8,128)(2,1)}, u32[]{:S(2)}) copy-start(bf16[64,512]{1,0:T(8,128)(2,1)} %get-tuple-element.864) | copy-start | bytes 196612
  61.5 26.8 %copy-start.6 = (f32[8,64]{1,0:T(8,128)S(1)}, f32[8,64]{1,0:T(8,128)}, u32[]{:S(2)}) copy-start(f32[8,64]{1,0:T(8,128)} %param.22) | copy-start | bytes 6148
  61.5 26.9 %copy-start.7 = (f32[1,1024]{1,0:T(1,128)S(1)}, f32[1,1024]{1,0:T(1,128)}, u32[]{:S(2)}) copy-start(f32[1,1024]{1,0:T(1,128)} %constant.278.clone.1) | copy-start | bytes 12292
  63.7 40.3 %all-to-all-start.1 = ((f32[32,1,8192]{2,1,0:T(1,128)}), f32[32,1,8192]{2,1,0:T(1,128)S(1)}, u32[]{:S(2)}, u32[]{:S(2)}) async-start(f32[32,1,8192]{2,1,0:T(1,128)} %reduce_sum.30), calls=%async_computation.1 | async-start | bytes 2097152 | tf_op jit(solution)/shard_map/all_to_all | solution.py:51
  74.0 14.4 %collective-permute-start.2 = (f32[3,256]{1,0:T(4,128)S(1)}, f32[3,256]{1,0:T(4,128)S(1)}, u32[]{:S(2)}, u32[]{:S(2)}) collective-permute-start(f32[3,256]{1,0:T(4,128)S(1)} %get-tuple-element.575), channel_id=1, source_target_pairs={{0,8},{8,16},{16,24},{24,32},{32,40},{40,48},{48,56},{56,64},{64,7... | collective-permute-start | bytes 9224 | tf_op jit(solution)/shard_map/ppermute | solution.py:28
  78.0 10.5 %collective-permute-start.3 = (f32[3,256]{1,0:T(4,128)S(1)}, f32[3,256]{1,0:T(4,128)S(1)}, u32[]{:S(2)}, u32[]{:S(2)}) collective-permute-start(f32[3,256]{1,0:T(4,128)S(1)} %get-tuple-element.574), channel_id=1, source_target_pairs={{8,0},{16,8},{24,16},{32,24},{40,32},{48,40},{56,48},{64,56},{72,6... | collective-permute-start | bytes 9224 | tf_op jit(solution)/shard_map/ppermute | solution.py:30
  79.9 8.6 %collective-permute-start = (bf16[64,256]{1,0:T(8,128)(2,1)S(1)}, bf16[64,256]{1,0:T(8,128)(2,1)S(1)}, u32[]{:S(2)}, u32[]{:S(2)}) collective-permute-start(bf16[64,256]{1,0:T(8,128)(2,1)S(1)} %get-tuple-element.569), channel_id=1, source_target_pairs={{0,8},{8,16},{16,24},{24,32},{32,40},{40,48},{48,56},{56,64},{64,7... | collective-permute-start | bytes 98312 | tf_op jit(solution)/shard_map/ppermute | solution.py:28
  83.6 5.7 %collective-permute-start.1 = (bf16[64,256]{1,0:T(8,128)(2,1)S(1)}, bf16[64,256]{1,0:T(8,128)(2,1)S(1)}, u32[]{:S(2)}, u32[]{:S(2)}) collective-permute-start(bf16[64,256]{1,0:T(8,128)(2,1)S(1)} %get-tuple-element.570), channel_id=1, source_target_pairs={{8,0},{16,8},{24,16},{32,24},{40,32},{48,40},{56,48},{64,56},{72,6... | collective-permute-start | bytes 98312 | tf_op jit(solution)/shard_map/ppermute | solution.py:30
  89.4 26.2 %copy-start.8 = (s32[4,4]{1,0:T(4,128)S(1)}, s32[4,4]{1,0:T(4,128)}, u32[]{:S(2)}) copy-start(s32[4,4]{1,0:T(4,128)} %param.19) | copy-start | bytes 196
  89.4 26.2 %copy-start.10 = (s32[4]{0:T(128)S(1)}, s32[4]{0:T(128)}, u32[]{:S(2)}) copy-start(s32[4]{0:T(128)} %param.20) | copy-start | bytes 52
  106.5 40.0 %all-to-all-start.2 = ((f32[32,1,8192]{2,1,0:T(1,128)}), f32[32,1,8192]{2,1,0:T(1,128)S(1)}, u32[]{:S(2)}, u32[]{:S(2)}) async-start(f32[32,1,8192]{2,1,0:T(1,128)} %broadcast_in_dim.126), calls=%async_computation.2 | async-start | bytes 2097152 | tf_op jit(solution)/shard_map/all_to_all | solution.py:61
  147.3 5.8 %copy-start.4 = (bf16[1024,64]{0,1:T(8,128)(2,1)S(1)}, bf16[1024,64]{0,1:T(8,128)(2,1)}, u32[]{:S(2)}) copy-start(bf16[1024,64]{0,1:T(8,128)(2,1)} %param.24) | copy-start | bytes 393220
  154.2 46.2 %all-to-all-start.5 = ((bf16[8,1024,64]{1,2,0:T(8,128)(2,1)}), bf16[8,1024,64]{1,2,0:T(8,128)(2,1)S(1)}, u32[]{:S(2)}, u32[]{:S(2)}) async-start(bf16[8,1024,64]{1,2,0:T(8,128)(2,1)} %broadcast_in_dim.129), calls=%async_computation.5 | async-start | bytes 2097152 | tf_op jit(solution)/shard_map/all_to_all | solution.py:61
  165.5 34.6 %copy-start.3 = (f32[64,512]{1,0:T(8,128)S(1)}, f32[64,512]{1,0:T(8,128)}, u32[]{:S(2)}) copy-start(f32[64,512]{1,0:T(8,128)} %get-tuple-element.438) | copy-start | bytes 393220
  165.5 45.1 %copy-start.5 = (bf16[64,1024]{1,0:T(8,128)(2,1)S(1)}, bf16[64,1024]{1,0:T(8,128)(2,1)}, u32[]{:S(2)}) copy-start(bf16[64,1024]{1,0:T(8,128)(2,1)} %param.25) | copy-start | bytes 393220
  200.1 15.2 %copy-start.9 = (f32[512]{0:T(512)S(1)}, f32[512]{0:T(512)}, u32[]{:S(2)}) copy-start(f32[512]{0:T(512)} %param.23) | copy-start | bytes 6148
  211.7 14.9 %all-to-all-start.6 = ((bf16[8,64,1024]{2,1,0:T(8,128)(2,1)}), bf16[8,64,1024]{2,1,0:T(8,128)(2,1)S(1)}, u32[]{:S(2)}, u32[]{:S(2)}) async-start(bf16[8,64,1024]{2,1,0:T(8,128)(2,1)} %broadcast_in_dim.130), calls=%async_computation.6 | async-start | bytes 2097152 | tf_op jit(solution)/shard_map/all_to_all | solution.py:61
where the time goes:
time: 232 us; the launch traced here: 228 us
  other arithmetic  75.6 us (33%)
  starting transfers between devices  51.8 us (22%)
  waiting for transfers between devices  35.8 us (15%)
  local copies, waits for them, and re-layouts  29.9 us (13%)
  matrix products  18.2 us (8%)
  blocking collectives  15.9 us (7%)
    another operation x4, other arithmetic  64.6 us
    all_to_all x3, waiting for transfers between devices, sent_to_all(): lax.all_to_all(jnp.broadcast_to(x[None], (size, *x.shape)), axis, 0, 0, t...  17.9 us
    all_to_all x3, starting transfers between devices, sent_to_all(): lax.all_to_all(jnp.broadcast_to(x[None], (size, *x.shape)), axis, 0, 0, t...  16.6 us
    all_to_all x1, waiting for transfers between devices, sum_by_axis(): return jnp.sum(lax.all_to_all(own, far, 0, 0, tiled=True), axis=0)  14.5 us
    all_to_all x1, starting transfers between devices, summed_on_arrival(): lax.all_to_all(pieces, axis, split_axis=0, concat_axis=0, tiled=True)  10.6 us
    all_to_all x1, starting transfers between devices, sum_by_axis(): return jnp.sum(lax.all_to_all(own, far, 0, 0, tiled=True), axis=0)  10.3 us
    all_to_all x1, blocking collectives, body(): lax.all_to_all(mixed, 'chan', split_axis=1, concat_axis=0, tiled=True)  10.1 us
    dot_general x2, matrix products, add_block(): jnp.dot(feature_rows, phases, preferred_element_type=jnp.float32)  8.16 us
  transfers between devices with their start and end apart: 9, of which 5 were waited for; matrix products, arithmetic and copies ran while one was open for 29% of the time, Pallas kernels for 0%

commit v1 on v0

v1 whole, which is shorter than its diff:
```python
import math

import jax
import jax.numpy as jnp
from jax import lax
from jax.experimental import pallas as pl
from jax.experimental.pallas import tpu as pltpu
from jax.sharding import PartitionSpec as P

MESH = pl.DeviceIdType.MESH
F32 = jnp.float32
BF16 = jnp.bfloat16

NZ = 8
NY = 4
NX = 4
NBRICK = NZ * NY * 2
NCHAN = 8
CD = 64
AD = 512
C = 512
HID = 1024
NB = 8
KS = 16
WIDTH, CROSS, CUTOFF, EPS = 4.0, 8.0, 2.0, 1e-06
SPACING = CUTOFF / (NB - 1)
INVERSE = 1.0 / math.sqrt(AD * NBRICK)

NN = (((1,), (0,)), ((), ()))
NT = (((1,), (1,)), ((), ()))


def dot(a, b, dims):
    return lax.dot_general(a, b, dims, preferred_element_type=F32)


def turn(u):
    u = u - jnp.floor(u + 0.5)
    th = u * math.pi
    q = th * th
    s = -1.0 / 39916800
    for n in (362880, -5040, 120, -6, 1):
        s = s * q + 1.0 / n
    s = s * th
    c = 1.0 / 479001600
    for n in (-3628800, 40320, -720, 24, -2, 1):
        c = c * q + 1.0 / n
    return 1.0 - 2.0 * s * s, 2.0 * s * c


def kernel(
    feat, pos, lists, counts, filt, rw, gain, win, wout, out,
    ph, trig, cxy, part, sib, ss, rs1, t2, rs2, fg, fq, flt,
    fe, pe, pt, sc, bas, msg, ew, wg, ms, mr,
    local_sem, halo_s, halo_r, core_s, core_r, rs1_s, rs1_r, rs2_s, rs2_r,
    ag1_s, ag1_r, ag2_s, ag2_r, fw_s, fw_r, w_s, w_r, wf_s, wf_r, a2a_s, a2a_r,
):
    brick = lax.axis_index("brick")
    chan = lax.axis_index("chan")
    core = lax.rem(brick, 2)
    z = lax.rem(brick // 2, NZ)
    y = brick // (2 * NZ)
    x = lax.rem(chan, NX)
    ylo = chan // NX
    first = core == 0
    second = core == 1

    def at(yy, zz, cc):
        return ((lax.rem(yy, NY) * NZ + lax.rem(zz, NZ)) * 2 + cc, chan)

    sibling = at(y, z, 1 - core)
    left = (lax.rem(brick + NBRICK - 1, NBRICK), chan)
    right = (lax.rem(brick + 1, NBRICK), chan)
    z_peer = lambda d: at(y, z + d, core)
    y_peer = lambda d: at(y + d, z, core)
    chan_peer = lambda d: (brick, lax.rem(chan + d, NCHAN))
    x_peer = lambda d: (brick, ylo * NX + lax.rem(x + d, NX))
    ylo_peer = (brick, (1 - ylo) * NX + x)

    barrier = pltpu.get_barrier_semaphore()
    partners = [z_peer(d) for d in range(1, NZ)] + [y_peer(d) for d in range(1, NY)]
    partners += [chan_peer(d) for d in range(1, NCHAN)] + [left, right]
    for device in partners:
        pl.semaphore_signal(barrier, inc=1, device_id=device, device_id_type=MESH)

    eye = (
        lax.broadcasted_iota(jnp.int32, (CD, CD), 0)
        == lax.broadcasted_iota(jnp.int32, (CD, CD), 1)
    ).astype(BF16)
    own = jnp.where(first, core * 32 + z * NY + y, y * NZ + z)
    filter_copy = pltpu.make_async_copy(
        filt.at[:, pl.ds(pl.multiple_of(own * 128, 128), 128)], flt, local_sem
    )
    filter_copy.start()
    win_t = dot(eye, win[...], NT).astype(BF16)
    wg[core, chan] = jnp.where(first, win_t, wout[...])
    fe[1] = feat[:, 0:256]
    fe[2] = feat[:, 256:512]
    for half in range(2):
        pe[1 + half] = jnp.zeros((8, 256), F32)
        pe[1 + half, 0:3, :] = pos[:, half * 256 : (half + 1) * 256]

    pl.semaphore_wait(barrier, len(partners))

    def remote(src, dst, send, recv, device):
        return pltpu.make_async_remote_copy(
            src_ref=src, dst_ref=dst, send_sem=send, recv_sem=recv,
            device_id=device, device_id_type=MESH,
        )

    halos = [
        remote(fe.at[1], fe.at[3], halo_s.at[0], halo_r.at[0], left),
        remote(fe.at[2], fe.at[0], halo_s.at[1], halo_r.at[1], right),
        remote(pe.at[1], pe.at[3], halo_s.at[2], halo_r.at[2], left),
        remote(pe.at[2], pe.at[0], halo_s.at[3], halo_r.at[3], right),
    ]
    for copy in halos:
        copy.start()

    mine = wg.at[core, chan]
    weight_y = remote(mine, mine, w_s.at[0], w_r.at[0], ylo_peer)
    weight_y.start()
    weight_x = [remote(mine, mine, w_s.at[d], w_r.at[d], x_peer(d)) for d in range(1, NX)]
    for copy in weight_x:
        copy.start()

    px, py, pz = pos[0:1, :], pos[1:2, :], pos[2:3, :]
    number = lax.broadcasted_iota(jnp.int32, (KS, 1), 0).astype(F32)
    xturn = (brick.astype(F32) + px) * (1.0 / NBRICK)
    cx, sx = turn((number + 1.0) * xturn)
    cy, sy = turn((number - KS // 2) * py)
    cz, sz = turn((number - KS // 2) * pz)
    trig[0], trig[1] = cz, sz
    for r in range(KS):
        rows = slice(r * KS, (r + 1) * KS)
        cxy[0, rows, :] = cx * cy[r : r + 1, :] - sx * sy[r : r + 1, :]
        cxy[1, rows, :] = sx * cy[r : r + 1, :] + cx * sy[r : r + 1, :]

    features = feat[...]

    def core_copy(i):
        return remote(part.at[i, 1 - core], sib.at[i], core_s.at[i], core_r.at[i], sibling)

    def compute(i):
        za = lax.rem(z + i + 1, NZ)
        yb = lax.rem(y + i // 2 + 1, NY)
        for half in range(2):
            na = 2 * za + half
            nb = 4 * yb + 2 * lax.rem(i, 2) + half
            ca, sa = trig[0, pl.ds(na, 1), :], trig[1, pl.ds(na, 1), :]
            cb, sb = trig[0, pl.ds(nb, 1), :], trig[1, pl.ds(nb, 1), :]
            for g in range(8):
                rows = slice(g * 32, (g + 1) * 32)
                cc, cs = cxy[0, rows, :], cxy[1, rows, :]
                ph[0, na, rows, :] = (cc * ca - cs * sa).astype(BF16)
                ph[1, nb, rows, :] = (cs * cb + cc * sb).astype(BF16)
            cols = slice(half * 256, (half + 1) * 256)
            part[i, 0, :, cols] = dot(features, ph[0, na], NT)
            part[i, 1, :, cols] = dot(features, ph[1, nb], NT)
        core_copy(i).start()

    def rs1_copy(i):
        device = (
            jnp.where(first, at(y, z + i + 1, 0)[0], at(y + i // 2 + 1, z, 1)[0]),
            chan,
        )
        return remote(ss.at[i], rs1.at[i], rs1_s.at[i], rs1_r.at[i], device)

    def finish(i):
        core_copy(i).wait_recv()
        ss[i] = (part[i, core] + sib[i]).astype(BF16)

        @pl.when(i < 7 - core)
        def _():
            rs1_copy(i).start()

    compute(0)

    def step(i, carry):
        compute(i)
        finish(i - 1)
        return carry

    lax.fori_loop(1, NZ, step, 0)
    finish(NZ - 1)

    weight_y.wait_recv()
    theirs = wg.at[core, (1 - ylo) * NX + x]
    weight_r = [
        remote(theirs, theirs, w_s.at[NX + d], w_r.at[NX + d], x_peer(d)) for d in range(1, NX)
    ]
    for copy in weight_r:
        copy.start()

    for copy in halos:
        copy.wait_recv()
    rw_pad = jnp.concatenate([rw[...], jnp.zeros((NB, CD), F32)], axis=1)
    rw_t = jnp.transpose(rw_pad)[0:CD, :]
    for e in range(8):
        lanes = slice((e % 2) * 128, (e % 2 + 1) * 128)
        shift = -1.0 if e < 2 else (1.0 if e >= 6 else 0.0)
        rows = pe[e // 2, :, lanes]
        at_x = lax.broadcasted_iota(jnp.int32, (8, 128), 0) == 0
        pt[e] = jnp.transpose(jnp.where(at_x, rows + shift, rows))
        block = fe[e // 2, :, lanes].astype(F32)
        for m in range(NB):
            sc[e, :, m * 128 : (m + 1) * 128] = (block * rw_t[:, m : m + 1]).astype(BF16)

    def pair(t, l):
        e = lists[t, l]
        used = jnp.where(l < counts[t], 1.0, 0.0).astype(F32)
        source = pt[e]
        half = t // 2
        lane = pl.ds(pl.multiple_of(lax.rem(t, 2) * 128, 128), 128)
        target = pe[1 + half, :, lane]
        dx = (source[:, 0:1] - target[0:1, :]) * WIDTH
        dy = (source[:, 1:2] - target[1:2, :]) * CROSS
        dz = (source[:, 2:3] - target[2:3, :]) * CROSS
        r2 = dx * dx + dy * dy + dz * dz
        env = jnp.maximum(1.0 - r2 * (1.0 / (CUTOFF * CUTOFF)), 0.0)
        tt = jnp.minimum(jnp.sqrt(r2) * (1.0 / SPACING), float(NB - 1))
        value = jnp.exp(-tt * tt) * (env * env * used)
        ratio = jnp.exp(2.0 * tt)
        bas[0:128, :] = value.astype(BF16)
        for m in range(1, NB):
            value = value * (ratio * math.exp(-(2 * m - 1)))
            bas[m * 128 : (m + 1) * 128, :] = value.astype(BF16)
        return dot(sc[e], bas[...], NN)

    def target_block(t, carry):
        total = lax.fori_loop(
            0, 4, lambda l, acc: acc + pair(t, l), jnp.zeros((CD, 128), F32)
        )
        msg[t] = total
        return carry

    lax.fori_loop(0, 4, target_block, 0)

    def rs2_copy(d):
        slot = jnp.where(first, lax.rem(y + d, NY), lax.rem(z + d, NZ))
        device = (jnp.where(first, at(y + d, z, 0)[0], at(y, z + d, 1)[0]), chan)
        return remote(t2.at[slot], rs2.at[d], rs2_s.at[d], rs2_r.at[d], device)

    ag_a = fg.at[0, pl.ds(z * NY, NY)]
    ag_b = fg.at[1, pl.ds(y * NZ, NZ)]

    @pl.when(first)
    def _():
        for i in range(NZ - 1):
            rs1_copy(i).wait_recv()
        total = ss[NZ - 1].astype(F32)
        for i in range(NZ - 1):
            total = total + rs1[i].astype(F32)
        for k in range(NY):
            t2[k] = total[:, k * 128 : (k + 1) * 128].astype(BF16)
        for d in range(1, NY):
            rs2_copy(d).start()
        for d in range(1, NY):
            rs2_copy(d).wait_recv()
        total = t2[y].astype(F32)
        for d in range(1, NY):
            total = total + rs2[d].astype(F32)
        fq[...] = total

    @pl.when(second)
    def _():
        for i in range(NZ - 2):
            rs1_copy(i).wait_recv()
        for half in range(2):
            total = ss[NZ - 2 + half].astype(F32)
            for i in range(NY - 1):
                total = total + rs1[2 * i + half].astype(F32)
            for k in range(4):
                t2[4 * half + k] = total[:, k * 128 : (k + 1) * 128].astype(BF16)
        for d in range(1, NZ):
            rs2_copy(d).start()
        for d in range(1, NZ):
            rs2_copy(d).wait_recv()
        total = t2[z].astype(F32)
        for d in range(1, NZ):
            total = total + rs2[d].astype(F32)
        fq[...] = total

    filter_copy.wait()
    fg[core, own] = (flt[...] * (fq[...] * INVERSE)).astype(BF16)

    def ag1_copy(d):
        block = fg.at[core, own]
        device = (jnp.where(first, at(y + d, z, 0)[0], at(y, z + d, 1)[0]), chan)
        return remote(block, block, ag1_s.at[d], ag1_r.at[d], device)

    def forward_copy(kind, group, slot):
        size = NY if kind == 0 else NZ
        block = fg.at[kind, pl.ds(group * size, size)]
        return remote(block, block, fw_s.at[slot], fw_r.at[slot], sibling)

    weights_on = remote(wg.at[core], wg.at[core], wf_s, wf_r, sibling)

    def weights_forward():
        for copy in weight_x + weight_r:
            copy.wait_recv()
        weights_on.start()

    def evaluate(kind, group):
        if kind == 0:
            blocks = [fg[0, group * NY + k] for k in range(NY)]
            phase = ph[0, pl.ds(2 * group, 2)].reshape(2 * 256, AD)
        else:
            blocks = [fg[1, group * NZ + k] for k in range(NZ)]
            phase = ph[1, pl.ds(4 * group, 4)].reshape(4 * 256, AD)
        ew[...] += dot(jnp.concatenate(blocks, axis=1), phase, NN)

    ew[...] = jnp.zeros((CD, AD), F32)

    def gather_and_evaluate(kind):
        near = NY if kind == 0 else NZ
        far = NZ if kind == 0 else NY
        here = z if kind == 0 else y
        block = ag_a if kind == 0 else ag_b
        other = 1 - kind
        far_here = y if kind == 0 else z
        for d in range(1, near):
            ag1_copy(d).start()
        weights_forward()
        for d in range(1, near):
            ag1_copy(d).wait_recv()
        peer = z_peer if kind == 0 else y_peer
        copies = [
            remote(block, block, ag2_s.at[d], ag2_r.at[d], peer(d)) for d in range(1, far)
        ]
        for copy in copies:
            copy.start()
        forward_copy(kind, here, 0).start()
        evaluate(kind, here)
        turns = far // (NZ + NY - far) if far > NY else 1
        given = 1 if far > NY else 2
        done = 0
        mine_back = y if kind == 0 else z
        for d in range(far):
            if d:
                copies[d - 1].wait_recv()
                group = lax.rem(here + far - d, far)
                forward_copy(kind, group, d).start()
                evaluate(kind, group)
            if (d + 1) % turns == 0:
                for _ in range(given):
                    group = lax.rem(mine_back + near - done, near)
                    forward_copy(other, group, done).wait_recv()
                    evaluate(other, group)
                    done += 1
        for copy in copies:
            copy.wait_send()
        for d in range(far):
            forward_copy(kind, here, d).wait_send()
        for d in range(1, near):
            ag1_copy(d).wait_send()
            rs2_copy(d).wait_send()

    @pl.when(first)
    def _():
        gather_and_evaluate(0)

    @pl.when(second)
    def _():
        gather_and_evaluate(1)

    for t in range(4):
        lanes = slice(t * 128, (t + 1) * 128)
        mixed = (
            features[:, lanes].astype(F32) + msg[t] + ew[:, lanes] * INVERSE
        ).astype(BF16)
        ms[2 * t] = mixed[:, 0:64]
        ms[2 * t + 1] = mixed[:, 64:128]
    exchange = []
    for d in range(1, NCHAN):
        device = chan_peer(d)
        exchange.append(
            remote(ms.at[device[1]], mr.at[chan], a2a_s.at[d], a2a_r.at[d], device)
        )
        exchange[-1].start()
    mr[chan] = ms[chan]
    remote(wg.at[1 - core], wg.at[1 - core], wf_s, wf_r, sibling).wait_recv()
    for copy in exchange:
        copy.wait_recv()

    values = mr[...].reshape(C, 64)
    values_t = dot(eye, values, NT)
    mean_square = jnp.sum(values_t * values_t, axis=1, keepdims=True) * (1.0 / C)
    normed = (values_t * lax.rsqrt(mean_square + EPS) * gain[...]).astype(BF16)
    hidden = dot(normed, wg[0].reshape(C, HID), NN)
    active = jax.nn.gelu(hidden).astype(BF16)
    mixed_out = dot(wg[1].reshape(C, HID), active, NT)
    out[...] = (values.astype(F32) + mixed_out).astype(BF16)

    for copy in halos + weight_x + weight_r + [weight_y, weights_on] + exchange:
        copy.wait_send()

    def sent(i, carry):
        core_copy(i).wait_send()

        @pl.when(i < 7 - core)
        def _():
            rs1_copy(i).wait_send()

        return carry

    lax.fori_loop(0, NZ, sent, 0)


def body(features, positions, lists, counts, fourier_filter, radial_weights, norm_gain, mlp_in, mlp_out):
    vmem = pl.BlockSpec(memory_space=pltpu.VMEM)
    smem = pl.BlockSpec(memory_space=pltpu.SMEM)
    dma = pltpu.SemaphoreType.DMA
    scratch = [
        pltpu.VMEM((2, KS, 256, AD), BF16),
        pltpu.VMEM((2, KS, AD), F32),
        pltpu.VMEM((2, 256, AD), F32),
        pltpu.VMEM((NZ, 2, CD, 512), F32),
        pltpu.VMEM((NZ, CD, 512), F32),
        pltpu.VMEM((NZ, CD, 512), BF16),
        pltpu.VMEM((NZ, CD, 512), BF16),
        pltpu.VMEM((NZ, CD, 128), BF16),
        pltpu.VMEM((NZ, CD, 128), BF16),
        pltpu.VMEM((2, 32, CD, 128), BF16),
        pltpu.VMEM((CD, 128), F32),
        pltpu.VMEM((CD, 128), F32),
        pltpu.VMEM((4, CD, 256), BF16),
        pltpu.VMEM((4, 8, 256), F32),
        pltpu.VMEM((8, 128, 8), F32),
        pltpu.VMEM((8, CD, NB * 128), BF16),
        pltpu.VMEM((NB * 128, 128), BF16),
        pltpu.VMEM((4, CD, 128), F32),
        pltpu.VMEM((CD, AD), F32),
        pltpu.VMEM((2, NCHAN, CD, HID), BF16),
        pltpu.VMEM((NCHAN, CD, 64), BF16),
        pltpu.VMEM((NCHAN, CD, 64), BF16),
        dma,
        dma((4,)), dma((4,)),
        dma((NZ,)), dma((NZ,)),
        dma((NZ,)), dma((NZ,)),
        dma((NZ,)), dma((NZ,)),
        dma((NZ,)), dma((NZ,)),
        dma((NZ,)), dma((NZ,)),
        dma((NZ,)), dma((NZ,)),
        dma((2 * NX,)), dma((2 * NX,)),
        dma, dma,
        dma((NCHAN,)), dma((NCHAN,)),
    ]
    return pl.pallas_call(
        kernel,
        out_shape=jax.ShapeDtypeStruct((C, 64), BF16),
        in_specs=[vmem, vmem, smem, smem, pl.BlockSpec(memory_space=pl.ANY), vmem, vmem, vmem, vmem],
        out_specs=vmem,
        scratch_shapes=scratch,
        compiler_params=pltpu.CompilerParams(
            collective_id=0, has_side_effects=True, vmem_limit_bytes=48 * 2**20
        ),
    )(
        features, positions, lists, counts, fourier_filter, radial_weights,
        norm_gain.reshape(1, C), mlp_in, mlp_out,
    )


def solution(mesh):
    return jax.shard_map(
        body,
        mesh=mesh,
        in_specs=(
            P("chan", "brick"),
            P(None, "brick"),
            P("brick", None),
            P("brick"),
            P("chan", None),
            P(None, "chan"),
            P(),
            P(None, "chan"),
            P("chan", None),
        ),
        out_specs=P(None, ("brick", "chan")),
        check_vma=False,
    )
```

time: 232 us -> 62.9 us (0.27); the launches traced: 228 us -> 62.7 us
  other arithmetic: 75.6 us -> 0 us
  Pallas kernels: 0 us -> 59.5 us
  starting transfers between devices: 51.8 us -> 0 us
  waiting for transfers between devices: 35.8 us -> 0 us
  local copies, waits for them, and re-layouts: 29.9 us -> 3.17 us
  matrix products: 18.2 us -> 0 us
  blocking collectives: 15.9 us -> 0 us
    another operation x4 -> x0, other arithmetic: 64.6 us -> none
    pallas_call x0 -> x1, Pallas kernels: none -> 59.5 us  [body(): pl.pallas_call(kernel, out_shape=jax.ShapeDtypeStruct((C, 64), BF16), in_...]
    all_to_all x5 -> x0, starting transfers between devices: 37.5 us -> none  [the longest x3 16.6 us: sent_to_all(): lax.all_to_all(jnp.broadcast_to(x[None], (size, *x.shape)), axis, 0, 0, t...]
    all_to_all x5 -> x0, waiting for transfers between devices: 35 us -> none  [the longest x3 17.9 us: sent_to_all(): lax.all_to_all(jnp.broadcast_to(x[None], (size, *x.shape)), axis, 0, 0, t...]
    dot_general x9 -> x0, matrix products: 18.2 us -> none  [the longest x2 8.16 us: add_block(): jnp.dot(feature_rows, phases, preferred_element_type=jnp.float32)]
    all_to_all x2 -> x0, blocking collectives: 15.9 us -> none  [the longest x1 10.1 us: body(): lax.all_to_all(mixed, 'chan', split_axis=1, concat_axis=0, tiled=True)]
    ppermute x4 -> x0, starting transfers between devices: 14.3 us -> none  [the longest x2 7.6 us: with_halo(): lax.ppermute(tail, axis, [(i, (i + 1) % count) for i in range(count)])]
    gather x16 -> x0, local copies, waits for them, and re-layouts: 9.68 us -> none  [the longest x4 2.98 us: one_target(): source = jnp.take(scaled_blocks, list_row, axis=2)]
  transfers between devices with their start and end apart: 9 -> 0, of which waited for: 5 -> 0; matrix products, arithmetic and copies ran while one was open for 29% -> 0% of each run, Pallas kernels for 0% -> 0%
where the time goes in v1:
time: 62.9 us; the launch traced here: 62.7 us
  Pallas kernels  59.5 us (95%)
  local copies, waits for them, and re-layouts  3.17 us (5%)
    pallas_call x1, Pallas kernels, body(): pl.pallas_call(kernel, out_shape=jax.ShapeDtypeStruct((C, 64), BF16), in_...  59.5 us
    unnamed x17, local copies, waits for them, and re-layouts  2.44 us

profile of v1, /device:TPU:1, one launch (start us, length us, event | category | flops | bytes accessed | tf_op | source)
XLA Modules:
  0.0 62.7 jit_solution(8071017415758314799)
XLA Ops:
  0.0 0.0 copy-start.1
  0.0 0.0 copy-start.2
  0.0 0.0 copy-start.3
  0.0 0.0 copy-start.4
  0.0 0.0 copy-start.5
  0.0 0.0 copy-start.6
  0.0 0.0 copy-start.7
  0.0 1.2 %copy.10.win = bf16[1024,64]{1,0:T(8,128)(2,1)S(1)} copy(bf16[1024,64]{0,1:T(8,128)(2,1)} %param.16) | data formatting | bytes 262144 | tf_op args[7]
  1.2 0.0 copy-done.1
  1.3 0.0 copy-done.2
  1.3 0.0 copy-done.3
  1.3 0.0 copy-done.4
  1.3 0.0 copy-done.5
  1.3 0.0 copy-done.6
  1.3 0.0 copy-done.7
  1.3 0.0 copy-start
  1.3 1.2 %copy-done = f32[64,4096]{1,0:T(8,128)S(1)} copy-done((f32[64,4096]{1,0:T(8,128)S(1)}, f32[64,4096]{1,0:T(8,128)}, u32[]{:S(2)}) %copy-start) | copy-done | bytes 1048600
  2.5 59.5 %shard_map.91 = bf16[512,64]{1,0:T(8,128)(2,1)S(1)} custom-call(bf16[64,512]{1,0:T(8,128)(2,1)S(1)} %copy-done.2, f32[3,512]{1,0:T(4,128)S(1)} %copy-done.3, s32[4,4]{1,0:T(4,128)S(1)} %copy-done.5, s32[4]{0:T(128)S(1)} %copy-done.7, f32[64,4096]{1,0:T(8,128)S(1)} %copy-done, f32[8,64]{1,0:T(8,128)S(1)} %copy-done.4, f32[1,512]{1,0:T(1,128)S(1)} %bitcast.1, ...), custom_call_target="tpu_custom_call" | custom-call | tf_op jit(solution)/shard_map/pallas_call | solution.py:449
  62.0 0.7 %copy.11 = bf16[512,64]{0,1:T(8,128)(2,1)} copy(bf16[512,64]{1,0:T(8,128)(2,1)S(1)} %shard_map.91) | data formatting | bytes 131072 | tf_op jit(solution)/shard_map/pallas_call | solution.py:449
Async XLA Ops:
  0.0 1.3 %copy-start.1 = (bf16[64,1024]{1,0:T(8,128)(2,1)S(1)}, bf16[64,1024]{1,0:T(8,128)(2,1)}, u32[]{:S(2)}) copy-start(bf16[64,1024]{1,0:T(8,128)(2,1)} %wout.1) | copy-start | bytes 393220
  0.0 1.3 %copy-start.2 = (bf16[64,512]{1,0:T(8,128)(2,1)S(1)}, bf16[64,512]{1,0:T(8,128)(2,1)}, u32[]{:S(2)}) copy-start(bf16[64,512]{1,0:T(8,128)(2,1)} %feat.1) | copy-start | bytes 196612
  0.0 1.3 %copy-start.3 = (f32[3,512]{1,0:T(4,128)S(1)}, f32[3,512]{1,0:T(4,128)}, u32[]{:S(2)}) copy-start(f32[3,512]{1,0:T(4,128)} %pos.1) | copy-start | bytes 18436
  0.0 1.3 %copy-start.4 = (f32[8,64]{1,0:T(8,128)S(1)}, f32[8,64]{1,0:T(8,128)}, u32[]{:S(2)}) copy-start(f32[8,64]{1,0:T(8,128)} %rw.1) | copy-start | bytes 6148
  0.0 1.3 %copy-start.5 = (s32[4,4]{1,0:T(4,128)S(1)}, s32[4,4]{1,0:T(4,128)}, u32[]{:S(2)}) copy-start(s32[4,4]{1,0:T(4,128)} %lists.1) | copy-start | bytes 196
  0.0 1.3 %copy-start.6 = (f32[512]{0:T(512)S(1)}, f32[512]{0:T(512)}, u32[]{:S(2)}) copy-start(f32[512]{0:T(512)} %param.15) | copy-start | bytes 6148
  0.0 1.3 %copy-start.7 = (s32[4]{0:T(128)S(1)}, s32[4]{0:T(128)}, u32[]{:S(2)}) copy-start(s32[4]{0:T(128)} %counts.1) | copy-start | bytes 52
  1.3 1.2 %copy-start = (f32[64,4096]{1,0:T(8,128)S(1)}, f32[64,4096]{1,0:T(8,128)}, u32[]{:S(2)}) copy-start(f32[64,4096]{1,0:T(8,128)} %filt.1) | copy-start | bytes 3145732

commit v2 on v1

v2 whole, which is shorter than its diff:
```python
import math

import jax
import jax.numpy as jnp
from jax import lax
from jax.experimental import pallas as pl
from jax.experimental.pallas import tpu as pltpu
from jax.sharding import PartitionSpec as P

MESH = pl.DeviceIdType.MESH
F32 = jnp.float32
BF16 = jnp.bfloat16

NZ = 8
NY = 4
NX = 4
NBRICK = NZ * NY * 2
NCHAN = 8
CD = 64
AD = 512
AC = 2 * AD
C = 512
HID = 1024
NB = 8
KS = 16
WAVES = 2
WIDTH, CROSS, CUTOFF, EPS = 4.0, 8.0, 2.0, 1e-06
SPACING = CUTOFF / (NB - 1)
INVERSE = 1.0 / math.sqrt(AD * NBRICK)

NN = (((1,), (0,)), ((), ()))
NT = (((1,), (1,)), ((), ()))


def dot(a, b, dims):
    return lax.dot_general(a, b, dims, preferred_element_type=F32)


def turn(u):
    u = u - jnp.floor(u + 0.5)
    th = u * math.pi
    q = th * th
    s = -1.0 / 39916800
    for n in (362880, -5040, 120, -6, 1):
        s = s * q + 1.0 / n
    s = s * th
    c = 1.0 / 479001600
    for n in (-3628800, 40320, -720, 24, -2, 1):
        c = c * q + 1.0 / n
    return 1.0 - 2.0 * s * s, 2.0 * s * c


def kernel(
    feat_in, pos_in, lists_in, counts_in, filt, rw_in, gain_in, win_in, wout_in, out,
    fc, pc, lists, counts, rw, gain,
    ph, trig, uv, ff, ss, own_sum, rs1, t2, rs2, fg, flt,
    pt, sc, bas, msg, ew, ewr, wg, ms, mr,
    load_sem, sib_s, sib_r, halo_s, halo_r, rs1_s, rs1_r, rs2_s, rs2_r,
    ag1_s, ag1_r, ag2_s, ag2_r, ew_s, ew_r, w_s, w_r, wf_s, wf_r, a2a_s, a2a_r,
):
    brick = lax.axis_index("brick")
    chan = lax.axis_index("chan")
    core = lax.rem(brick, 2)
    z = lax.rem(brick // 2, NZ)
    y = brick // (2 * NZ)
    x = lax.rem(chan, NX)
    ylo = chan // NX
    first = core == 0
    second = core == 1
    kinds = ((0, first), (1, second))

    def at(yy, zz, cc):
        return ((lax.rem(yy, NY) * NZ + lax.rem(zz, NZ)) * 2 + cc, chan)

    sibling = at(y, z, 1 - core)
    beside = (lax.rem(brick + NBRICK + 2 * core - 1, NBRICK), chan)
    z_peer = lambda d: at(y, z + d, core)
    y_peer = lambda d: at(y + d, z, core)
    chan_peer = lambda d: (brick, lax.rem(chan + d, NCHAN))
    x_peer = lambda d: (brick, ylo * NX + lax.rem(x + d, NX))
    ylo_peer = (brick, (1 - ylo) * NX + x)

    barrier = pltpu.get_barrier_semaphore()
    partners = [z_peer(d) for d in range(1, NZ)] + [y_peer(d) for d in range(1, NY)]
    partners += [chan_peer(d) for d in range(1, NCHAN)] + [sibling, beside]
    for device in partners:
        pl.semaphore_signal(barrier, inc=1, device_id=device, device_id_type=MESH)

    loads = [(lists_in, lists), (counts_in, counts), (rw_in, rw), (gain_in, gain)]
    for pair_at in range(2):
        lanes = pl.ds(pair_at * 256, 256)
        loads.append((feat_in.at[:, lanes], fc.at[1 + 2 * core + pair_at]))
        loads.append((pos_in.at[:, lanes], pc.at[1 + 2 * core + pair_at]))
    own_unit = jnp.where(first, y, lax.rem(z, 4))
    own_nz = [jnp.where(first, 2 * z + w, 4 * y + 2 * w + z // 4) for w in range(WAVES)]
    for w in range(WAVES):
        rows = pl.ds(pl.multiple_of(lax.rem(own_unit, 2) * 32, 32), 32)
        lanes = pl.ds(pl.multiple_of(own_nz[w] * 256 + own_unit // 2 * 128, 128), 128)
        loads.append((filt.at[rows, lanes], flt.at[w]))
    loads = [pltpu.make_async_copy(a, b, load_sem.at[i]) for i, (a, b) in enumerate(loads)]
    for copy in loads:
        copy.start()
    weight_load = load_sem.at[len(loads)]

    @pl.when(first)
    def _():
        pltpu.make_async_copy(win_in, wg.at[core, chan], weight_load).start()

    @pl.when(second)
    def _():
        pltpu.make_async_copy(wout_in, wg.at[core, chan], weight_load).start()

    for copy in loads:
        copy.wait()
    pltpu.make_async_copy(wout_in, wg.at[core, chan], weight_load).wait()

    pl.semaphore_wait(barrier, len(partners))

    def remote(src, dst, send, recv, device):
        return pltpu.make_async_remote_copy(
            src_ref=src, dst_ref=dst, send_sem=send, recv_sem=recv,
            device_id=device, device_id_type=MESH,
        )

    places = pc.at[pl.ds(1 + 2 * core, 2)]
    block = fc.at[pl.ds(1 + 2 * core, 2)]
    to_sibling = [
        remote(places, places, sib_s.at[0], sib_r.at[0], sibling),
        remote(block, block, sib_s.at[1], sib_r.at[1], sibling),
    ]
    rim, land = jnp.where(first, 1, 4), jnp.where(first, 5, 0)
    halos = [
        remote(pc.at[rim], pc.at[land], halo_s.at[0], halo_r.at[0], beside),
        remote(fc.at[rim], fc.at[land], halo_s.at[1], halo_r.at[1], beside),
    ]
    mine = wg.at[core, chan]
    weight_y = remote(mine, mine, w_s.at[0], w_r.at[0], ylo_peer)
    weight_x = [remote(mine, mine, w_s.at[d], w_r.at[d], x_peer(d)) for d in range(1, NX)]
    for copy in to_sibling + halos + [weight_y] + weight_x:
        copy.start()

    number = lax.broadcasted_iota(jnp.int32, (KS, 1), 0).astype(F32)

    def dimension_phases(half):
        where = 1 + 2 * half
        for pair_at in range(2):
            spot = pc[where + pair_at]
            lanes = pl.ds(pl.multiple_of(half * 512 + pair_at * 256, 256), 256)
            px, py, pz = spot[0:1, :], spot[1:2, :], spot[2:3, :]
            xturn = ((brick - core + half).astype(F32) + px) * (1.0 / NBRICK)
            cx, sx = turn((number + 1.0) * xturn)
            cy, sy = turn((number - KS // 2) * py)
            cz, sz = turn((number - KS // 2) * pz)
            trig[0, :, lanes] = cz
            trig[1, :, lanes] = sz
            for r in range(KS):
                rows = slice(r * KS, (r + 1) * KS)
                even = cx * cy[r : r + 1, :] - sx * sy[r : r + 1, :]
                odd = sx * cy[r : r + 1, :] + cx * sy[r : r + 1, :]
                uv[0, rows, lanes] = jnp.where(first, even, odd)
                uv[1, rows, lanes] = jnp.where(first, -odd, even)

    dimension_phases(core)
    to_sibling[0].wait_recv()
    dimension_phases(1 - core)
    to_sibling[1].wait_recv()
    for pair_at in range(4):
        ff[:, pair_at * 256 : (pair_at + 1) * 256] = fc[1 + pair_at]
    features = ff[...]

    def rs1_copy(w, i):
        device = (
            jnp.where(first, at(y, z + i + 1, 0)[0], at(y + i // 2 + 1, z, 1)[0]),
            chan,
        )
        slot = w * NZ + i
        return remote(ss.at[slot], rs1.at[slot], rs1_s.at[slot], rs1_r.at[slot], device)

    def forward(step, carry):
        w, i = step // NZ, lax.rem(step, NZ)
        za = lax.rem(z + i + 1, NZ)
        yb = lax.rem(y + i // 2 + 1, NY)
        nz = jnp.where(first, 2 * za + w, 4 * yb + 2 * w + lax.rem(i, 2))
        cn, sn = trig[0, pl.ds(nz, 1), :], trig[1, pl.ds(nz, 1), :]
        for g in range(16):
            rows = slice(g * 16, (g + 1) * 16)
            ph[nz, rows, :] = (uv[0, rows, :] * cn + uv[1, rows, :] * sn).astype(BF16)
        total = dot(features, ph[nz], NT)
        ss[step] = total.astype(BF16)

        @pl.when(i < 7 - core)
        def _():
            rs1_copy(w, i).start()

        @pl.when(i >= 6)
        def _():
            own_sum[2 * w + i - 6] = total

        return carry

    lax.fori_loop(0, WAVES * NZ, forward, 0)

    weight_y.wait_recv()
    theirs = wg.at[core, (1 - ylo) * NX + x]
    weight_r = [
        remote(theirs, theirs, w_s.at[NX + d], w_r.at[NX + d], x_peer(d)) for d in range(1, NX)
    ]
    for copy in weight_r:
        copy.start()

    def make_sources():
        for copy in halos:
            copy.wait_recv()
        rw_pad = jnp.concatenate([rw[...], jnp.zeros((NB, CD), F32)], axis=1)
        rw_t = jnp.transpose(rw_pad)[0:CD, :]
        for e in range(8):
            lanes = slice((e % 2) * 128, (e % 2 + 1) * 128)
            shift = -1.0 if e < 2 else (1.0 if e >= 6 else 0.0)
            rows = jnp.concatenate(
                [pc[2 * core + e // 2, :, lanes], jnp.zeros((5, 128), F32)], axis=0
            )
            at_x = lax.broadcasted_iota(jnp.int32, (8, 128), 0) == 0
            pt[e] = jnp.transpose(jnp.where(at_x, rows + shift, rows))
            block = fc[2 * core + e // 2, :, lanes].astype(F32)
            for m in range(NB):
                sc[e, :, m * 128 : (m + 1) * 128] = (block * rw_t[:, m : m + 1]).astype(BF16)

    def message(t, l):
        e = lists[t, l]
        used = jnp.where(l < counts[t], 1.0, 0.0).astype(F32)
        source = pt[e]
        lane = slice((t % 2) * 128, (t % 2 + 1) * 128)
        target = pc[1 + 2 * core + t // 2, :, lane]
        dx = (source[:, 0:1] - target[0:1, :]) * WIDTH
        dy = (source[:, 1:2] - target[1:2, :]) * CROSS
        dz = (source[:, 2:3] - target[2:3, :]) * CROSS
        r2 = dx * dx + dy * dy + dz * dz
        env = jnp.maximum(1.0 - r2 * (1.0 / (CUTOFF * CUTOFF)), 0.0)
        tt = jnp.minimum(jnp.sqrt(r2) * (1.0 / SPACING), float(NB - 1))
        value = jnp.exp(-tt * tt) * (env * env * used)
        ratio = jnp.exp(2.0 * tt)
        bas[0:128, :] = value.astype(BF16)
        for m in range(1, NB):
            value = value * (ratio * math.exp(-(2 * m - 1)))
            bas[m * 128 : (m + 1) * 128, :] = value.astype(BF16)
        return dot(sc[e], bas[...], NN)

    def messages(t):
        msg[t] = lax.fori_loop(
            0, 4, lambda l, acc: acc + message(t, l), jnp.zeros((CD, 128), F32)
        )

    near = (NY, NZ)
    far = (NZ, NY)

    def near_device(d):
        return (jnp.where(first, at(y + d, z, 0)[0], at(y, z + d, 1)[0]), chan)

    def rs2_copy(w, d):
        unit = jnp.where(first, lax.rem(y + d, NY), lax.rem(z + d, NZ))
        slot = w * NZ + d
        return remote(
            t2.at[w, unit], rs2.at[slot], rs2_s.at[slot], rs2_r.at[slot], near_device(d)
        )

    def far_summed(w):
        for kind, here in kinds:

            @pl.when(here)
            def _():
                for i in range(NZ - 1 - kind):
                    rs1_copy(w, i).wait_recv()
                for h in range(1 + kind):
                    total = own_sum[2 * w + (h if kind else 1)]
                    for i in range(h, NZ - 1 - kind, 1 + kind):
                        total = total + rs1[w * NZ + i].astype(F32)
                    for u in range(4):
                        t2[w, 4 * h + u] = total[
                            32 * (u % 2) : 32 * (u % 2 + 1), 128 * (u // 2) : 128 * (u // 2 + 1)
                        ].astype(BF16)
                for d in range(1, near[kind]):
                    rs2_copy(w, d).start()

    def ag1_copy(w, d):
        unit = fg.at[own_nz[w], own_unit]
        slot = w * NZ + d
        return remote(unit, unit, ag1_s.at[slot], ag1_r.at[slot], near_device(d))

    def near_summed(w):
        for kind, here in kinds:

            @pl.when(here)
            def _():
                total = t2[w, z if kind else y].astype(F32)
                for d in range(1, near[kind]):
                    rs2_copy(w, d).wait_recv()
                    total = total + rs2[w * NZ + d].astype(F32)
                fg[own_nz[w], own_unit] = (flt[w] * (total * INVERSE)).astype(BF16)
                for d in range(1, near[kind]):
                    ag1_copy(w, d).start()

    def ag2_copy(kind, w, d):
        if kind == 0:
            group = fg.at[pl.ds(2 * z + w, 1)]
        else:
            group = fg.at[pl.ds(4 * y + 2 * w, 2)]
        slot = w * NZ + d
        device = (y_peer if kind else z_peer)(d)
        return remote(group, group, ag2_s.at[slot], ag2_r.at[slot], device)

    def near_gathered(w):
        for kind, here in kinds:

            @pl.when(here)
            def _():
                for d in range(1, near[kind]):
                    ag1_copy(w, d).wait_recv()
                for d in range(1, far[kind]):
                    ag2_copy(kind, w, d).start()

    def product(nz):
        top = jnp.concatenate([fg[nz, 0], fg[nz, 2]], axis=1)
        bottom = jnp.concatenate([fg[nz, 1], fg[nz, 3]], axis=1)
        return dot(jnp.concatenate([top, bottom], axis=0), ph[nz], NN)

    def evaluate(w, begin):
        for kind, here in kinds:

            @pl.when(here)
            def _():
                for i in range(4):
                    if kind == 0:
                        chunks = []
                        for d in (2 * i, 2 * i + 1):
                            if d:
                                ag2_copy(kind, w, d).wait_recv()
                            chunks.append(2 * lax.rem(z + NZ - d, NZ) + w)
                    else:
                        if i:
                            ag2_copy(kind, w, i).wait_recv()
                        base = 4 * lax.rem(y + NY - i, NY) + 2 * w
                        chunks = [base, base + 1]
                    total = product(chunks[0]) + product(chunks[1])
                    if begin and i == 0:
                        ew[0] = total[:, 0:AD]
                        ew[1] = total[:, AD:AC]
                    else:
                        ew[0] += total[:, 0:AD]
                        ew[1] += total[:, AD:AC]

    weights_on = remote(wg.at[core], wg.at[core], wf_s, wf_r, sibling)

    make_sources()
    far_summed(0)
    messages(0)
    far_summed(1)
    near_summed(0)
    messages(1)
    near_summed(1)
    near_gathered(0)
    messages(2)
    near_gathered(1)
    for copy in weight_x + weight_r:
        copy.wait_recv()
    weights_on.start()
    messages(3)
    evaluate(0, True)
    evaluate(1, False)

    ewald_share = remote(ew.at[1 - core], ewr, ew_s, ew_r, sibling)
    ewald_share.start()

    ewald_share.wait_recv()
    for t in range(4):
        lanes = slice(t * 128, (t + 1) * 128)
        pair_lanes = slice((t % 2) * 128, (t % 2 + 1) * 128)
        ewald = (ew[core, :, lanes] + ewr[:, lanes]) * INVERSE
        mixed = (
            fc[1 + 2 * core + t // 2, :, pair_lanes].astype(F32) + msg[t] + ewald
        ).astype(BF16)
        ms[2 * t] = mixed[:, 0:64]
        ms[2 * t + 1] = mixed[:, 64:128]
    exchange = []
    for d in range(1, NCHAN):
        device = chan_peer(d)
        exchange.append(
            remote(ms.at[device[1]], mr.at[chan], a2a_s.at[d], a2a_r.at[d], device)
        )
        exchange[-1].start()
    mr[chan] = ms[chan]
    remote(wg.at[1 - core], wg.at[1 - core], wf_s, wf_r, sibling).wait_recv()
    for copy in exchange:
        copy.wait_recv()

    eye = (
        lax.broadcasted_iota(jnp.int32, (64, 64), 0)
        == lax.broadcasted_iota(jnp.int32, (64, 64), 1)
    ).astype(BF16)
    values = dot(eye, mr[...].reshape(C, 64), NT)
    mean_square = jnp.sum(values * values, axis=1, keepdims=True) * (1.0 / C)
    normed = (values * lax.rsqrt(mean_square + EPS) * gain[...]).astype(BF16)
    hidden = dot(normed, wg[0].reshape(C, HID), NN)
    active = jax.nn.gelu(hidden).astype(BF16)
    out[...] = (values + dot(active, wg[1].reshape(C, HID), NT)).astype(BF16)

    for copy in to_sibling + halos + weight_x + weight_r + [weight_y, weights_on, ewald_share]:
        copy.wait_send()
    for copy in exchange:
        copy.wait_send()
    for kind, here in kinds:

        @pl.when(here)
        def _():
            for w in range(WAVES):
                for i in range(NZ - 1 - kind):
                    rs1_copy(w, i).wait_send()
                for d in range(1, near[kind]):
                    rs2_copy(w, d).wait_send()
                    ag1_copy(w, d).wait_send()
                for d in range(1, far[kind]):
                    ag2_copy(kind, w, d).wait_send()


def body(features, positions, lists, counts, fourier_filter, radial_weights, norm_gain, mlp_in, mlp_out):
    dma = pltpu.SemaphoreType.DMA
    slots = WAVES * NZ
    scratch = [
        pltpu.VMEM((6, CD, 256), BF16),
        pltpu.VMEM((6, 3, 256), F32),
        pltpu.SMEM((4, 4), jnp.int32),
        pltpu.SMEM((4,), jnp.int32),
        pltpu.VMEM((NB, CD), F32),
        pltpu.VMEM((1, C), F32),
        pltpu.VMEM((KS, 256, AC), BF16),
        pltpu.VMEM((2, KS, AC), F32),
        pltpu.VMEM((2, 256, AC), F32),
        pltpu.VMEM((CD, AC), BF16),
        pltpu.VMEM((slots, CD, 256), BF16),
        pltpu.VMEM((2 * WAVES, CD, 256), F32),
        pltpu.VMEM((slots, CD, 256), BF16),
        pltpu.VMEM((WAVES, NZ, 32, 128), BF16),
        pltpu.VMEM((slots, 32, 128), BF16),
        pltpu.VMEM((KS, 4, 32, 128), BF16),
        pltpu.VMEM((WAVES, 32, 128), F32),
        pltpu.VMEM((8, 128, 8), F32),
        pltpu.VMEM((8, CD, NB * 128), BF16),
        pltpu.VMEM((NB * 128, 128), BF16),
        pltpu.VMEM((4, CD, 128), F32),
        pltpu.VMEM((2, CD, AD), F32),
        pltpu.VMEM((CD, AD), F32),
        pltpu.VMEM((2, NCHAN, CD, HID), BF16),
        pltpu.VMEM((NCHAN, CD, 64), BF16),
        pltpu.VMEM((NCHAN, CD, 64), BF16),
        dma((11,)),
        dma((2,)), dma((2,)),
        dma((2,)), dma((2,)),
        dma((slots,)), dma((slots,)),
        dma((slots,)), dma((slots,)),
        dma((slots,)), dma((slots,)),
        dma((slots,)), dma((slots,)),
        dma, dma,
        dma((2 * NX,)), dma((2 * NX,)),
        dma, dma,
        dma((NCHAN,)), dma((NCHAN,)),
    ]
    return pl.pallas_call(
        kernel,
        out_shape=jax.ShapeDtypeStruct((64, C), BF16),
        in_specs=[pl.BlockSpec(memory_space=pltpu.HBM)] * 9,
        out_specs=pl.BlockSpec(memory_space=pltpu.VMEM),
        scratch_shapes=scratch,
        compiler_params=pltpu.CompilerParams(
            collective_id=0, has_side_effects=True, vmem_limit_bytes=60 * 2**20
        ),
    )(
        features, positions, lists, counts, fourier_filter, radial_weights,
        norm_gain.reshape(1, C), mlp_in.T, mlp_out,
    ).T


def solution(mesh):
    return jax.shard_map(
        body,
        mesh=mesh,
        in_specs=(
            P("chan", "brick"),
            P(None, "brick"),
            P("brick", None),
            P("brick"),
            P("chan", None),
            P(None, "chan"),
            P(),
            P(None, "chan"),
            P("chan", None),
        ),
        out_specs=P(None, ("brick", "chan")),
        check_vma=False,
    )
```

time: 62.9 us -> 53 us (0.84)
  Pallas kernels: 59.5 us -> 51.3 us
  local copies, waits for them, and re-layouts: 3.17 us -> 1.47 us
    pallas_call x1, Pallas kernels: 59.5 us -> 51.3 us  [body(): pl.pallas_call(kernel, out_shape=jax.ShapeDtypeStruct((64, C), BF16), in_...]
    unnamed x17 -> x1, local copies, waits for them, and re-layouts: 2.44 us -> 1.47 us
    pallas_call x1 -> x0, local copies, waits for them, and re-layouts: 0.73 us -> none  [body(): pl.pallas_call(kernel, out_shape=jax.ShapeDtypeStruct((C, 64), BF16), in_...]
where the time goes in v2:
time: 53 us; the launch traced here: 52.8 us
  Pallas kernels  51.3 us (97%)
  local copies, waits for them, and re-layouts  1.47 us (3%)
    pallas_call x1, Pallas kernels, body(): pl.pallas_call(kernel, out_shape=jax.ShapeDtypeStruct((64, C), BF16), in_...  51.3 us
    unnamed x1, local copies, waits for them, and re-layouts  1.47 us

profile of v2, /device:TPU:1, one launch (start us, length us, event | category | flops | bytes accessed | tf_op | source)
XLA Modules:
  0.0 52.8 jit_solution(17696020108219083798)
XLA Ops:
  0.0 51.3 %shard_map.91 = bf16[64,512]{1,0:T(8,128)(2,1)} custom-call(bf16[64,512]{1,0:T(8,128)(2,1)} %feat_in.1, f32[3,512]{1,0:T(4,128)} %pos_in.1, s32[4,4]{1,0:T(4,128)} %lists_in.1, s32[4]{0:T(128)} %counts_in.1, f32[64,4096]{1,0:T(8,128)} %filt.1, f32[8,64]{1,0:T(8,128)} %rw_in.1, f32[1,512]{1,0:T(1,128)} %bitcast.5, bf16[64,1024]{1,0:T(8,128)(2,1)} %bitcast.4, ...), custom_call_target="tpu_custom_call" | custom-call | tf_op jit(solution)/shard_map/pallas_call | solution.py:466
  51.3 1.5 %copy.11 = bf16[512,64]{0,1:T(8,128)(2,1)} copy(bf16[512,64]{0,1:T(8,128)(2,1)} %bitcast.3) | data formatting | bytes 131072

commit v3 on v2

--- a/solution.py
+++ b/solution.py
@@ -18,7 +18,6 @@
 NCHAN = 8
 CD = 64
 AD = 512
-AC = 2 * AD
 C = 512
 HID = 1024
 NB = 8
@@ -30,6 +29,11 @@
 
 NN = (((1,), (0,)), ((), ()))
 NT = (((1,), (1,)), ((), ()))
+
+
+FAR_Z = (4, 3, 5, 2, 6, 1, 7)
+FAR_Y = (2, 1, 3)
+FAR_CHAN = ((1, 2), (1, 1), (1, 3), (0, 2), (1, 0), (0, 1), (0, 3))
 
 
 def dot(a, b, dims):
@@ -80,17 +84,14 @@
     x_peer = lambda d: (brick, ylo * NX + lax.rem(x + d, NX))
     ylo_peer = (brick, (1 - ylo) * NX + x)
 
-    barrier = pltpu.get_barrier_semaphore()
-    partners = [z_peer(d) for d in range(1, NZ)] + [y_peer(d) for d in range(1, NY)]
-    partners += [chan_peer(d) for d in range(1, NCHAN)] + [sibling, beside]
-    for device in partners:
-        pl.semaphore_signal(barrier, inc=1, device_id=device, device_id_type=MESH)
-
-    loads = [(lists_in, lists), (counts_in, counts), (rw_in, rw), (gain_in, gain)]
+    loads = []
     for pair_at in range(2):
         lanes = pl.ds(pair_at * 256, 256)
+        loads.append((pos_in.at[:, lanes], pc.at[1 + 2 * core + pair_at]))
         loads.append((feat_in.at[:, lanes], fc.at[1 + 2 * core + pair_at]))
-        loads.append((pos_in.at[:, lanes], pc.at[1 + 2 * core + pair_at]))
+        loads.append((feat_in.at[:, lanes], ff.at[core, :, lanes]))
+    urgent = len(loads)
+    loads += [(lists_in, lists), (counts_in, counts), (rw_in, rw), (gain_in, gain)]
     own_unit = jnp.where(first, y, lax.rem(z, 4))
     own_nz = [jnp.where(first, 2 * z + w, 4 * y + 2 * w + z // 4) for w in range(WAVES)]
     for w in range(WAVES):
@@ -110,42 +111,18 @@
     def _():
         pltpu.make_async_copy(wout_in, wg.at[core, chan], weight_load).start()
 
-    for copy in loads:
-        copy.wait()
-    pltpu.make_async_copy(wout_in, wg.at[core, chan], weight_load).wait()
-
-    pl.semaphore_wait(barrier, len(partners))
-
-    def remote(src, dst, send, recv, device):
-        return pltpu.make_async_remote_copy(
-            src_ref=src, dst_ref=dst, send_sem=send, recv_sem=recv,
-            device_id=device, device_id_type=MESH,
-        )
-
-    places = pc.at[pl.ds(1 + 2 * core, 2)]
-    block = fc.at[pl.ds(1 + 2 * core, 2)]
-    to_sibling = [
-        remote(places, places, sib_s.at[0], sib_r.at[0], sibling),
-        remote(block, block, sib_s.at[1], sib_r.at[1], sibling),
-    ]
-    rim, land = jnp.where(first, 1, 4), jnp.where(first, 5, 0)
-    halos = [
-        remote(pc.at[rim], pc.at[land], halo_s.at[0], halo_r.at[0], beside),
-        remote(fc.at[rim], fc.at[land], halo_s.at[1], halo_r.at[1], beside),
-    ]
-    mine = wg.at[core, chan]
-    weight_y = remote(mine, mine, w_s.at[0], w_r.at[0], ylo_peer)
-    weight_x = [remote(mine, mine, w_s.at[d], w_r.at[d], x_peer(d)) for d in range(1, NX)]
-    for copy in to_sibling + halos + [weight_y] + weight_x:
-        copy.start()
+    barrier = pltpu.get_barrier_semaphore()
+    partners = [sibling, beside] + [z_peer(d) for d in FAR_Z] + [y_peer(d) for d in FAR_Y]
+    partners += [chan_peer(d) for d in range(1, NCHAN)]
+    for device in partners:
+        pl.semaphore_signal(barrier, inc=1, device_id=device, device_id_type=MESH)
 
     number = lax.broadcasted_iota(jnp.int32, (KS, 1), 0).astype(F32)
 
     def dimension_phases(half):
-        where = 1 + 2 * half
         for pair_at in range(2):
-            spot = pc[where + pair_at]
-            lanes = pl.ds(pl.multiple_of(half * 512 + pair_at * 256, 256), 256)
+            spot = pc[1 + 2 * half + pair_at]
+            lanes = pl.ds(pl.multiple_of(half * AD + pair_at * 256, 256), 256)
             px, py, pz = spot[0:1, :], spot[1:2, :], spot[2:3, :]
             xturn = ((brick - core + half).astype(F32) + px) * (1.0 / NBRICK)
             cx, sx = turn((number + 1.0) * xturn)
@@ -160,17 +137,60 @@
                 uv[0, rows, lanes] = jnp.where(first, even, odd)
                 uv[1, rows, lanes] = jnp.where(first, -odd, even)
 
+    def z_ahead(i):
+        return 4 + jnp.where(lax.rem(i, 2) == 1, -((i + 1) // 2), i // 2)
+
+    def y_ahead(i):
+        k = i // 2
+        return 2 + jnp.where(lax.rem(k, 2) == 1, -((k + 1) // 2), k // 2)
+
+    def wave_number(step):
+        w, i = step // NZ, lax.rem(step, NZ)
+        za = lax.rem(z + z_ahead(i), NZ)
+        yb = lax.rem(y + y_ahead(i), NY)
+        return jnp.where(first, 2 * za + w, 4 * yb + 2 * w + lax.rem(i, 2))
+
+    for copy in loads[:urgent]:
+        copy.wait()
+    for copy in loads[urgent:]:
+        copy.wait()
+    pltpu.make_async_copy(wout_in, wg.at[core, chan], weight_load).wait()
+
+    pl.semaphore_wait(barrier, len(partners))
+
+    def remote(src, dst, send, recv, device):
+        return pltpu.make_async_remote_copy(
+            src_ref=src, dst_ref=dst, send_sem=send, recv_sem=recv,
+            device_id=device, device_id_type=MESH,
+        )
+
+    places = pc.at[pl.ds(1 + 2 * core, 2)]
+    near_rim = 2 + core
+    to_sibling = [
+        remote(places, places, sib_s.at[0], sib_r.at[0], sibling),
+        remote(ff.at[core], ff.at[core], sib_s.at[1], sib_r.at[1], sibling),
+        remote(fc.at[near_rim], fc.at[near_rim], sib_s.at[2], sib_r.at[2], sibling),
+    ]
+    rim, land = jnp.where(first, 1, 4), jnp.where(first, 5, 0)
+    halos = [
+        remote(pc.at[rim], pc.at[land], halo_s.at[0], halo_r.at[0], beside),
+        remote(fc.at[rim], fc.at[land], halo_s.at[1], halo_r.at[1], beside),
+    ]
+    mine = wg.at[core, chan]
+    weight_y = remote(mine, mine, w_s.at[0], w_r.at[0], ylo_peer)
+    weight_x = [remote(mine, mine, w_s.at[d], w_r.at[d], x_peer(d)) for d in range(1, NX)]
+    for copy in to_sibling + halos + [weight_y] + weight_x:
+        copy.start()
+
     dimension_phases(core)
     to_sibling[0].wait_recv()
     dimension_phases(1 - core)
     to_sibling[1].wait_recv()
-    for pair_at in range(4):
-        ff[:, pair_at * 256 : (pair_at + 1) * 256] = fc[1 + pair_at]
-    features = ff[...]
+    features = jnp.concatenate([ff[0], ff[1]], axis=1)
 
     def rs1_copy(w, i):
         device = (
-            jnp.where(first, at(y, z + i + 1, 0)[0], at(y + i // 2 + 1, z, 1)[0]),
+            jnp.where(first, at(y, z + z_ahead(i), 0)[0], at(y + y_ahead(i), z, 1)[0]),
             chan,
         )
         slot = w * NZ + i
@@ -178,9 +198,7 @@
 
     def forward(step, carry):
         w, i = step // NZ, lax.rem(step, NZ)
-        za = lax.rem(z + i + 1, NZ)
-        yb = lax.rem(y + i // 2 + 1, NY)
-        nz = jnp.where(first, 2 * za + w, 4 * yb + 2 * w + lax.rem(i, 2))
+        nz = wave_number(step)
         cn, sn = trig[0, pl.ds(nz, 1), :], trig[1, pl.ds(nz, 1), :]
         for g in range(16):
             rows = slice(g * 16, (g + 1) * 16)
@@ -209,8 +227,9 @@
         copy.start()
 
     def make_sources():
-        for copy in halos:
+        for copy in halos + to_sibling[2:]:
             copy.wait_recv()
+        msg[...] = jnp.zeros((4, CD, 128), F32)
         rw_pad = jnp.concatenate([rw[...], jnp.zeros((NB, CD), F32)], axis=1)
         rw_t = jnp.transpose(rw_pad)[0:CD, :]
         for e in range(8):
@@ -229,7 +248,7 @@
         e = lists[t, l]
         used = jnp.where(l < counts[t], 1.0, 0.0).astype(F32)
         source = pt[e]
-        lane = slice((t % 2) * 128, (t % 2 + 1) * 128)
+        lane = pl.ds(pl.multiple_of(lax.rem(t, 2) * 128, 128), 128)
         target = pc[1 + 2 * core + t // 2, :, lane]
         dx = (source[:, 0:1] - target[0:1, :]) * WIDTH
         dy = (source[:, 1:2] - target[1:2, :]) * CROSS
@@ -245,13 +264,16 @@
             bas[m * 128 : (m + 1) * 128, :] = value.astype(BF16)
         return dot(sc[e], bas[...], NN)
 
-    def messages(t):
-        msg[t] = lax.fori_loop(
-            0, 4, lambda l, acc: acc + message(t, l), jnp.zeros((CD, 128), F32)
-        )
-
-    near = (NY, NZ)
-    far = (NZ, NY)
+    def messages(begin, end):
+        def entry(k, carry):
+            t = k // 4
+            msg[t] += message(t, lax.rem(k, 4))
+            return carry
+
+        lax.fori_loop(begin, end, entry, 0)
+
+    near = (FAR_Y, FAR_Z)
+    far = (FAR_Z, FAR_Y)
 
     def near_device(d):
         return (jnp.where(first, at(y + d, z, 0)[0], at(y, z + d, 1)[0]), chan)
@@ -278,7 +300,7 @@
                         t2[w, 4 * h + u] = total[
                             32 * (u % 2) : 32 * (u % 2 + 1), 128 * (u // 2) : 128 * (u // 2 + 1)
                         ].astype(BF16)
-                for d in range(1, near[kind]):
+                for d in near[kind]:
                     rs2_copy(w, d).start()
 
     def ag1_copy(w, d):
@@ -292,11 +314,11 @@
             @pl.when(here)
             def _():
                 total = t2[w, z if kind else y].astype(F32)
-                for d in range(1, near[kind]):
+                for d in near[kind]:
                     rs2_copy(w, d).wait_recv()
                     total = total + rs2[w * NZ + d].astype(F32)
                 fg[own_nz[w], own_unit] = (flt[w] * (total * INVERSE)).astype(BF16)
-                for d in range(1, near[kind]):
+                for d in near[kind]:
                     ag1_copy(w, d).start()
 
     def ag2_copy(kind, w, d):
@@ -313,17 +335,19 @@
 
             @pl.when(here)
             def _():
-                for d in range(1, near[kind]):
+                for d in near[kind]:
                     ag1_copy(w, d).wait_recv()
-                for d in range(1, far[kind]):
+                for d in far[kind]:
                     ag2_copy(kind, w, d).start()
 
-    def product(nz):
+    def filtered(nz):
         top = jnp.concatenate([fg[nz, 0], fg[nz, 2]], axis=1)
         bottom = jnp.concatenate([fg[nz, 1], fg[nz, 3]], axis=1)
-        return dot(jnp.concatenate([top, bottom], axis=0), ph[nz], NN)
-
-    def evaluate(w, begin):
+        return jnp.concatenate([top, bottom], axis=0)
+
+    ewald_share = remote(ew.at[1 - core], ewr, ew_s, ew_r, sibling)
+
+    def evaluate(w):
         for kind, here in kinds:
 
             @pl.when(here)
@@ -331,43 +355,43 @@
                 for i in range(4):
                     if kind == 0:
                         chunks = []
-                        for d in (2 * i, 2 * i + 1):
+                        for d in ((0, 1), (7, 2), (6, 3), (5, 4))[i]:
                             if d:
                                 ag2_copy(kind, w, d).wait_recv()
                             chunks.append(2 * lax.rem(z + NZ - d, NZ) + w)
                     else:
-                        if i:
-                            ag2_copy(kind, w, i).wait_recv()
-                        base = 4 * lax.rem(y + NY - i, NY) + 2 * w
+                        d = (0, 1, 3, 2)[i]
+                        if d:
+                            ag2_copy(kind, w, d).wait_recv()
+                        base = 4 * lax.rem(y + NY - d, NY) + 2 * w
                         chunks = [base, base + 1]
-                    total = product(chunks[0]) + product(chunks[1])
-                    if begin and i == 0:
-                        ew[0] = total[:, 0:AD]
-                        ew[1] = total[:, AD:AC]
-                    else:
-                        ew[0] += total[:, 0:AD]
-                        ew[1] += total[:, AD:AC]
+                    total = sum(dot(filtered(nz), ph[nz], NN) for nz in chunks)
+                    for half in range(2):
+                        lanes = slice(half * AD, (half + 1) * AD)
+                        if w == 0 and i == 0:
+                            ew[half] = total[:, lanes]
+                        else:
+                            ew[half] += total[:, lanes]
 
     weights_on = remote(wg.at[core], wg.at[core], wf_s, wf_r, sibling)
 
     make_sources()
     far_summed(0)
-    messages(0)
+    messages(0, 3)
     far_summed(1)
+    messages(3, 6)
     near_summed(0)
-    messages(1)
+    messages(6, 10)
     near_summed(1)
+    messages(10, 13)
     near_gathered(0)
-    messages(2)
+    messages(13, 16)
     near_gathered(1)
     for copy in weight_x + weight_r:
         copy.wait_recv()
     weights_on.start()
-    messages(3)
-    evaluate(0, True)
-    evaluate(1, False)
-
-    ewald_share = remote(ew.at[1 - core], ewr, ew_s, ew_r, sibling)
+    evaluate(0)
+    evaluate(1)
     ewald_share.start()
 
     ewald_share.wait_recv()
@@ -381,10 +405,10 @@
         ms[2 * t] = mixed[:, 0:64]
         ms[2 * t + 1] = mixed[:, 64:128]
     exchange = []
-    for d in range(1, NCHAN):
-        device = chan_peer(d)
+    for i, (dy, dx) in enumerate(FAR_CHAN):
+        device = (brick, lax.rem(ylo + dy, 2) * NX + lax.rem(x + dx, NX))
         exchange.append(
-            remote(ms.at[device[1]], mr.at[chan], a2a_s.at[d], a2a_r.at[d], device)
+            remote(ms.at[device[1]], mr.at[chan], a2a_s.at[i], a2a_r.at[i], device)
         )
         exchange[-1].start()
     mr[chan] = ms[chan]
@@ -414,10 +438,10 @@
             for w in range(WAVES):
                 for i in range(NZ - 1 - kind):
                     rs1_copy(w, i).wait_send()
-                for d in range(1, near[kind]):
+                for d in near[kind]:
                     rs2_copy(w, d).wait_send()
                     ag1_copy(w, d).wait_send()
-                for d in range(1, far[kind]):
+                for d in far[kind]:
                     ag2_copy(kind, w, d).wait_send()
 
 
@@ -431,10 +455,10 @@
         pltpu.SMEM((4,), jnp.int32),
         pltpu.VMEM((NB, CD), F32),
         pltpu.VMEM((1, C), F32),
-        pltpu.VMEM((KS, 256, AC), BF16),
-        pltpu.VMEM((2, KS, AC), F32),
-        pltpu.VMEM((2, 256, AC), F32),
-        pltpu.VMEM((CD, AC), BF16),
+        pltpu.VMEM((KS, 256, 2 * AD), BF16),
+        pltpu.VMEM((2, KS, 2 * AD), F32),
+        pltpu.VMEM((2, 256, 2 * AD), F32),
+        pltpu.VMEM((2, CD, AD), BF16),
         pltpu.VMEM((slots, CD, 256), BF16),
         pltpu.VMEM((2 * WAVES, CD, 256), F32),
         pltpu.VMEM((slots, CD, 256), BF16),
@@ -451,8 +475,8 @@
         pltpu.VMEM((2, NCHAN, CD, HID), BF16),
         pltpu.VMEM((NCHAN, CD, 64), BF16),
         pltpu.VMEM((NCHAN, CD, 64), BF16),
-        dma((11,)),
-        dma((2,)), dma((2,)),
+        dma((13,)),
+        dma((3,)), dma((3,)),
         dma((2,)), dma((2,)),
         dma((slots,)), dma((slots,)),
         dma((slots,)), dma((slots,)),

time: 53 us -> 51.9 us (0.979)
  Pallas kernels: 51.3 us -> 50.2 us
    pallas_call x1, Pallas kernels: 51.3 us -> 50.2 us  [body(): pl.pallas_call(kernel, out_shape=jax.ShapeDtypeStruct((64, C), BF16), in_...]
where the time goes in v3:
time: 51.9 us; the launch traced here: 51.7 us
  Pallas kernels  50.2 us (97%)
  local copies, waits for them, and re-layouts  1.47 us (3%)
    pallas_call x1, Pallas kernels, body(): pl.pallas_call(kernel, out_shape=jax.ShapeDtypeStruct((64, C), BF16), in_...  50.2 us
    unnamed x1, local copies, waits for them, and re-layouts  1.47 us

profile of v3, /device:TPU:1, one launch (start us, length us, event | category | flops | bytes accessed | tf_op | source)
XLA Modules:
  0.0 51.7 jit_solution(6986404756996842132)
XLA Ops:
  0.0 50.2 %shard_map.91 = bf16[64,512]{1,0:T(8,128)(2,1)} custom-call(bf16[64,512]{1,0:T(8,128)(2,1)} %feat_in.1, f32[3,512]{1,0:T(4,128)} %pos_in.1, s32[4,4]{1,0:T(4,128)} %lists_in.1, s32[4]{0:T(128)} %counts_in.1, f32[64,4096]{1,0:T(8,128)} %filt.1, f32[8,64]{1,0:T(8,128)} %rw_in.1, f32[1,512]{1,0:T(1,128)} %bitcast.5, bf16[64,1024]{1,0:T(8,128)(2,1)} %bitcast.4, ...), custom_call_target="tpu_custom_call" | custom-call | tf_op jit(solution)/shard_map/pallas_call | solution.py:490
  50.2 1.5 %copy.11 = bf16[512,64]{0,1:T(8,128)(2,1)} copy(bf16[512,64]{0,1:T(8,128)(2,1)} %bitcast.3) | data formatting | bytes 131072

commit v4 on v3

--- a/solution.py
+++ b/solution.py
@@ -152,9 +152,6 @@
 
     for copy in loads[:urgent]:
         copy.wait()
-    for copy in loads[urgent:]:
-        copy.wait()
-    pltpu.make_async_copy(wout_in, wg.at[core, chan], weight_load).wait()
 
     pl.semaphore_wait(barrier, len(partners))
 
@@ -179,10 +176,15 @@
     mine = wg.at[core, chan]
     weight_y = remote(mine, mine, w_s.at[0], w_r.at[0], ylo_peer)
     weight_x = [remote(mine, mine, w_s.at[d], w_r.at[d], x_peer(d)) for d in range(1, NX)]
-    for copy in to_sibling + halos + [weight_y] + weight_x:
+    for copy in to_sibling + halos:
         copy.start()
 
     dimension_phases(core)
+    for copy in loads[urgent:]:
+        copy.wait()
+    pltpu.make_async_copy(wout_in, wg.at[core, chan], weight_load).wait()
+    for copy in [weight_y] + weight_x:
+        copy.start()
     to_sibling[0].wait_recv()
     dimension_phases(1 - core)
     to_sibling[1].wait_recv()
@@ -365,7 +367,17 @@
                             ag2_copy(kind, w, d).wait_recv()
                         base = 4 * lax.rem(y + NY - d, NY) + 2 * w
                         chunks = [base, base + 1]
-                    total = sum(dot(filtered(nz), ph[nz], NN) for nz in chunks)
+                    sides = [filtered(nz) for nz in chunks]
+                    if w == WAVES - 1 and i == 3:
+                        for half in (1 - core, core):
+                            lanes = pl.ds(pl.multiple_of(half * AD, AD), AD)
+                            ew[half] += sum(
+                                dot(a, ph[nz, :, lanes], NN) for a, nz in zip(sides, chunks)
+                            )
+                            if half is not core:
+                                ewald_share.start()
+                        continue
+                    total = sum(dot(a, ph[nz], NN) for a, nz in zip(sides, chunks))
                     for half in range(2):
                         lanes = slice(half * AD, (half + 1) * AD)
                         if w == 0 and i == 0:
@@ -387,12 +399,11 @@
     near_gathered(0)
     messages(13, 16)
     near_gathered(1)
+    evaluate(0)
     for copy in weight_x + weight_r:
         copy.wait_recv()
     weights_on.start()
-    evaluate(0)
     evaluate(1)
-    ewald_share.start()
 
     ewald_share.wait_recv()
     for t in range(4):

time: 51.9 us -> 52.4 us (level)
  Pallas kernels: 50.2 us -> 50.8 us
    pallas_call x1, Pallas kernels: 50.2 us -> 50.8 us  [body(): pl.pallas_call(kernel, out_shape=jax.ShapeDtypeStruct((64, C), BF16), in_...]
where the time goes in v4:
time: 52.4 us; the launch traced here: 52.3 us
  Pallas kernels  50.8 us (97%)
  local copies, waits for them, and re-layouts  1.47 us (3%)
    pallas_call x1, Pallas kernels, body(): pl.pallas_call(kernel, out_shape=jax.ShapeDtypeStruct((64, C), BF16), in_...  50.8 us
    unnamed x1, local copies, waits for them, and re-layouts  1.47 us

profile of v4, /device:TPU:1, one launch (start us, length us, event | category | flops | bytes accessed | tf_op | source)
XLA Modules:
  0.0 52.3 jit_solution(6455270844061655413)
XLA Ops:
  0.0 50.8 %shard_map.91 = bf16[64,512]{1,0:T(8,128)(2,1)} custom-call(bf16[64,512]{1,0:T(8,128)(2,1)} %feat_in.1, f32[3,512]{1,0:T(4,128)} %pos_in.1, s32[4,4]{1,0:T(4,128)} %lists_in.1, s32[4]{0:T(128)} %counts_in.1, f32[64,4096]{1,0:T(8,128)} %filt.1, f32[8,64]{1,0:T(8,128)} %rw_in.1, f32[1,512]{1,0:T(1,128)} %bitcast.5, bf16[64,1024]{1,0:T(8,128)(2,1)} %bitcast.4, ...), custom_call_target="tpu_custom_call" | custom-call | tf_op jit(solution)/shard_map/pallas_call | solution.py:501
  50.8 1.5 %copy.11 = bf16[512,64]{0,1:T(8,128)(2,1)} copy(bf16[512,64]{0,1:T(8,128)(2,1)} %bitcast.3) | data formatting | bytes 131072
